TPU v7x, 512 devices: a whole 4x4x16 slice. The times are simulated.
512 devices in a mesh: sec: 4 (over x), seq: 32 (over z, core), tp: 4 (over y).
Axes of the slice: x: 4, y: 4, z: 16, core: 2. Of those that a mesh axis runs over, the one named last changes fastest.
Arguments:
- text_embed: bfloat16 [32768, 8192], P(('sec', 'seq'), 'tp'), may hold values from -6 to 6
- image_rows: bfloat16 [16384, 8192], P(('sec', 'seq'), 'tp'), may hold values from -6 to 6
- token_source: int32 [32768], P(('sec', 'seq')), may hold values from -1 to 16383, as said below
- slot_dest: int32 [16384], P(('sec', 'seq')), may hold values from -1 to 32767, as said below
- norm_gain: float32 [8192], P('tp'), may hold values from 0.1 to 1.9
- kv_weight: bfloat16 [1024, 8192], P(('sec', 'seq'), 'tp'), may hold values from -0.0625 to 0.0625
- kv_cot: bfloat16 [32768, 1024], P(('sec', 'seq'), 'tp'), may hold values from -6 to 6
Outputs:
- key_value: bfloat16 [32768, 1024], P(('sec', 'seq'), 'tp')
- text_grad: bfloat16 [32768, 8192], P(('sec', 'seq'), 'tp')
- image_grads: bfloat16 [16384, 8192], P(('sec', 'seq'), 'tp')
Inputs may be any that keep to these rules, and one draw needn't show every extreme that they name: Encoder device e's slot s has index e * 128 + s; token_source and slot_dest are inverse to each other. The slots of one encoder device that fill tokens of one device's 256 tokens stand in the order of those tokens, at most 2 of them, and in every draw some encoder device fills exactly 2 tokens of some device. `slot_dest`: the inverse of token_source.
All inputs are finite; a program needn't handle non-finite values.
Results may differ from a plain program's by a relative error of at most 0.0049.
Values may be sent and summed in bfloat16 or wider, within the bound.
A program may use at most 64 MiB of HBM per device.

v0:
```python
import jax
import jax.numpy as jnp
from jax import lax
from jax.sharding import PartitionSpec as P

D = 8192


epsilon = 1e-06


def place_rank(owner, peer_count):
    peers = jnp.arange(peer_count, dtype=jnp.int32)
    onehot = (owner[:, None] == peers[None, :]).astype(jnp.int32)
    before = jnp.cumsum(onehot, axis=0) - onehot
    return jnp.sum(before * onehot, axis=1)


def per_device(text_embed, image_rows, token_source, slot_dest, norm_gain, kv_weight, kv_cot):
    tok_count = text_embed.shape[0]
    slot_count = image_rows.shape[0]
    feat_count = text_embed.shape[1]
    sec_count = lax.axis_size("sec")
    seq_count = lax.axis_size("seq")
    peer_count = sec_count * seq_count
    capacity = tok_count // peer_count
    buffer_rows = peer_count * capacity
    filled = slot_dest >= 0
    target = jnp.where(filled, slot_dest // tok_count, -1)
    send_rank = place_rank(target, peer_count)
    send_pos = jnp.where(filled, target * capacity + send_rank, buffer_rows)
    send_rows = (
        jnp.zeros((buffer_rows, feat_count), jnp.bfloat16).at[send_pos].set(image_rows, mode="drop")
    )
    received = lax.all_to_all(send_rows, ("sec", "seq"), split_axis=0, concat_axis=0, tiled=True)
    is_image = token_source >= 0
    anchor = jnp.where(is_image, token_source // slot_count, -1)
    recv_rank = place_rank(anchor, peer_count)
    take_pos = jnp.where(is_image, anchor * capacity + recv_rank, 0)
    picked = jnp.take(received, take_pos, axis=0)
    mixed = jnp.where(is_image[:, None], picked, text_embed)
    hidden = mixed.astype(jnp.float32)
    sumsq = lax.psum(jnp.sum(hidden * hidden, axis=1), "tp")
    scale = lax.rsqrt(sumsq / D + epsilon)
    normed = (hidden * scale[:, None] * norm_gain).astype(jnp.bfloat16)
    partial_value = lax.dot_general(
        normed,
        lax.all_gather(kv_weight, ("sec", "seq"), axis=0, tiled=True),
        (((1,), (1,)), ((), ())),
        preferred_element_type=jnp.float32,
    )
    key_value = lax.psum_scatter(partial_value, "tp", scatter_dimension=1, tiled=True).astype(
        jnp.bfloat16
    )
    cot_all = lax.all_gather(kv_cot, "tp", axis=1, tiled=True)
    normed_grad = jnp.dot(
        cot_all,
        lax.all_gather(kv_weight, ("sec", "seq"), axis=0, tiled=True),
        preferred_element_type=jnp.float32,
    )
    scaled_grad = norm_gain * normed_grad
    dots = lax.psum(jnp.sum(scaled_grad * hidden, axis=1), "tp")
    input_grad = scale[:, None] * scaled_grad - hidden * (scale * scale * scale * dots / D)[:, None]
    grad_rows = input_grad.astype(jnp.bfloat16)
    text_grad = jnp.where(is_image[:, None], jnp.zeros_like(grad_rows), grad_rows)
    back_pos = jnp.where(is_image, take_pos, buffer_rows)
    back_rows = (
        jnp.zeros((buffer_rows, feat_count), jnp.bfloat16).at[back_pos].set(grad_rows, mode="drop")
    )
    returned = lax.all_to_all(back_rows, ("sec", "seq"), split_axis=0, concat_axis=0, tiled=True)
    slot_grads = jnp.take(returned, jnp.where(filled, send_pos, 0), axis=0)
    image_grads = jnp.where(filled[:, None], slot_grads, jnp.zeros_like(slot_grads))
    return (key_value, text_grad, image_grads)


def solution(mesh):
    return jax.shard_map(
        per_device,
        mesh=mesh,
        in_specs=(
            P(("sec", "seq"), "tp"),
            P(("sec", "seq"), "tp"),
            P(("sec", "seq")),
            P(("sec", "seq")),
            P("tp"),
            P(("sec", "seq"), "tp"),
            P(("sec", "seq"), "tp"),
        ),
        out_specs=(P(("sec", "seq"), "tp"), P(("sec", "seq"), "tp"), P(("sec", "seq"), "tp")),
        check_vma=False,
    )
```

profile of v0, /device:TPU:1, one launch (start us, length us, event | category | flops | bytes accessed | tf_op | source)
XLA Modules:
  0.0 261.1 jit_solution(8509682652797544374)
XLA Ops:
  7.2 0.7 all-gather.2.cloned.1.call-update
  7.9 0.7 fusion.23
  9.0 0.7 compare_select_fusion.3
  9.7 2.2 scatter_custom_fusion
  11.9 1.5 all_to_all.16
  13.4 20.4 %all-to-all-start = ((bf16[128,2,2048]{2,1,0:T(2,128)(2,1)}), bf16[128,2,2048]{2,1,0:T(2,128)(2,1)S(1)}, u32[]{:S(2)}, u32[]{:S(2)}) async-start(bf16[128,2,2048]{2,1,0:T(2,128)(2,1)} %all_to_all.16), calls=%async_computation | async-start | bytes 2097152 | tf_op jit(solution)/shard_map/all_to_all | solution.py:35
  34.5 12.5 %all_gather.8 = bf16[256,1024]{1,0:T(8,128)(2,1)} all-gather(bf16[256,256]{1,0:T(8,128)(2,1)S(1)} %copy-done), channel_id=1, replica_groups=mesh['sec'=4,'seq'=32,'tp'=4] {'tp'}, dimensions={1}, use_global_device_ids=true | all-gather | bytes 655360 | tf_op jit(solution)/shard_map/all_gather | solution.py:55
  47.0 43.4 %all-to-all-done = bf16[128,2,2048]{2,1,0:T(2,128)(2,1)S(1)} async-done(((bf16[128,2,2048]{2,1,0:T(2,128)(2,1)}), bf16[128,2,2048]{2,1,0:T(2,128)(2,1)S(1)}, u32[]{:S(2)}, u32[]{:S(2)}) %all-to-all-start) | async-done | bytes 1048608 | tf_op jit(solution)/shard_map/all_to_all | solution.py:35
  90.4 0.4 all_to_all.18
  90.8 2.3 gather_fusion
  93.1 72.2 %all-gather.2.cloned.1.call-done = bf16[1024,2048]{1,0:T(8,128)(2,1)} async-done(((bf16[8,2048]{1,0:T(8,128)(2,1)}), bf16[1024,2048]{1,0:T(8,128)(2,1)}) %all-gather.2.cloned.1.call-update) | async-done | bytes 4194320 | tf_op jit(solution)/shard_map/all_gather | solution.py:48
  165.4 4.6 %fusion.3 = (f32[256]{0:T(256)S(1)}, f32[256]{0:T(256)S(1)}, bf16[256,2048]{1,0:T(8,128)(2,1)S(1)}, f32[256,2048]{1,0:T(8,128)S(1)}) fusion(bf16[256,2048]{1,0:T(8,128)(2,1)} %param.7, bf16[256,2048]{1,0:T(8,128)(2,1)} %gather_fusion, pred[256]{0:T(512)(128)(4,1)S(1)} %get-tuple-element.12, pred[256]{0:T(512)(128)(4,1)S(1)} %get-tuple-element.15, ...), kind=kOutput, calls=%fused_computation.12 | convolution fusion | flops 1077935616 | bytes 9972224 | tf_op jit(solution)/shard_map/dot_general | solution.py:56
  169.9 8.5 %all-reduce = (f32[256]{0:T(256)S(1)}, f32[256]{0:T(256)S(1)}) all-reduce(f32[256]{0:T(256)S(1)} %get-tuple-element.4, f32[256]{0:T(256)S(1)} %get-tuple-element.3), channel_id=1, replica_groups=mesh['sec'=4,'seq'=32,'tp'=4] {'tp'}, use_global_device_ids=true, to_apply=%region_7.8 | all-reduce | flops 512 | bytes 4096 | tf_op jit(solution)/shard_map/psum | solution.py:43
  178.4 1.8 broadcast_select_fusion
  180.2 3.1 %scatter_custom_fusion.1 = bf16[256,2048]{1,0:T(8,128)(2,1)S(1)} fusion(s32[256]{0:T(256)S(1)} %compare_select_fusion, bf16[256,2048]{1,0:T(8,128)(2,1)} %get-tuple-element.10, bf16[]{:T(256)} %constant.77.clone.1), kind=kCustom, calls=%fused_computation.21 | custom fusion | bytes 1049088 | tf_op jit(solution)/shard_map/scatter | solution.py:68
  183.3 1.5 all_to_all.19
  184.8 12.8 %all-to-all-start.1 = ((bf16[128,2,2048]{2,1,0:T(2,128)(2,1)}), bf16[128,2,2048]{2,1,0:T(2,128)(2,1)S(1)}, u32[]{:S(2)}, u32[]{:S(2)}) async-start(bf16[128,2,2048]{2,1,0:T(2,128)(2,1)} %all_to_all.19), calls=%async_computation.2 | async-start | bytes 2097152 | tf_op jit(solution)/shard_map/all_to_all | solution.py:70
  197.7 4.5 %fusion.6 = f32[256,1024]{1,0:T(8,128)} fusion(bf16[1024,2048]{1,0:T(8,128)(2,1)} %all-gather.2.cloned.1.call-done, bf16[256,2048]{1,0:T(8,128)(2,1)S(1)} %get-tuple-element.11, f32[2048]{0:T(1024)S(1)} %copy-done.3, f32[256]{0:T(256)S(1)} %get-tuple-element.17), kind=kOutput, calls=%fused_computation.15 | convolution fusion | flops 1075838976 | bytes 6300672 | tf_op jit(solution)/shard_map/dot_general | solution.py:46
  202.3 28.7 %reduce-scatter.2.cloned.1.call-done = f32[256,256]{1,0:T(8,128)} async-done(((f32[256,1024]{1,0:T(8,128)}), f32[256,256]{1,0:T(8,128)}) %reduce-scatter.2.cloned.1.call-update) | async-done | bytes 262160 | tf_op jit(solution)/shard_map/reduce_scatter | solution.py:52
  231.0 1.6 convert_element_type.27
  232.6 19.4 %all-to-all-done.1 = bf16[128,2,2048]{2,1,0:T(2,128)(2,1)S(1)} async-done(((bf16[128,2,2048]{2,1,0:T(2,128)(2,1)}), bf16[128,2,2048]{2,1,0:T(2,128)(2,1)S(1)}, u32[]{:S(2)}, u32[]{:S(2)}) %all-to-all-start.1) | async-done | bytes 1048608 | tf_op jit(solution)/shard_map/all_to_all | solution.py:70
  252.0 0.4 all_to_all.21
  252.4 0.9 gather_fusion.1
  253.4 0.9 select_select_fusion.1
  (30 shorter events, 1.2 us)
Async XLA Ops:
  7.2 158.2 %all-gather.2.cloned.1.call-start = ((), (), s32[]{:S(2)}) async-start(), calls=%async_computation.3 | async-start | bytes 4227072 | tf_op jit(solution)/shard_map/all_gather | solution.py:48
  11.9 21.9 %copy-start.1 = (s32[256]{0:T(256)S(1)}, s32[256]{0:T(256)}, u32[]{:S(2)}) copy-start(s32[256]{0:T(256)} %param.9) | copy-start | bytes 3076
  11.9 22.6 %copy-start = (bf16[256,256]{1,0:T(8,128)(2,1)S(1)}, bf16[256,256]{1,0:T(8,128)(2,1)}, u32[]{:S(2)}) copy-start(bf16[256,256]{1,0:T(8,128)(2,1)} %param.13) | copy-start | bytes 393220
  13.4 77.0 %all-to-all-start = ((bf16[128,2,2048]{2,1,0:T(2,128)(2,1)}), bf16[128,2,2048]{2,1,0:T(2,128)(2,1)S(1)}, u32[]{:S(2)}, u32[]{:S(2)}) async-start(bf16[128,2,2048]{2,1,0:T(2,128)(2,1)} %all_to_all.16), calls=%async_computation | async-start | bytes 2097152 | tf_op jit(solution)/shard_map/all_to_all | solution.py:35
  90.8 74.6 %copy-start.3 = (f32[2048]{0:T(1024)S(1)}, f32[2048]{0:T(1024)}, u32[]{:S(2)}) copy-start(f32[2048]{0:T(1024)} %param.11) | copy-start | bytes 24580
  184.8 67.2 %all-to-all-start.1 = ((bf16[128,2,2048]{2,1,0:T(2,128)(2,1)}), bf16[128,2,2048]{2,1,0:T(2,128)(2,1)S(1)}, u32[]{:S(2)}, u32[]{:S(2)}) async-start(bf16[128,2,2048]{2,1,0:T(2,128)(2,1)} %all_to_all.19), calls=%async_computation.2 | async-start | bytes 2097152 | tf_op jit(solution)/shard_map/all_to_all | solution.py:70
  197.6 4.6 %copy-start.2 = (s32[128]{0:T(128)S(1)}, s32[128]{0:T(128)}, u32[]{:S(2)}) copy-start(s32[128]{0:T(128)} %param.10) | copy-start | bytes 1540
  197.7 33.4 %reduce-scatter.2.cloned.1.call-start = ((), (), s32[]{:S(2)}) async-start(), calls=%async_computation.4 | async-start | bytes 1310720 | tf_op jit(solution)/shard_map/reduce_scatter | solution.py:52
Sparse Core Ops, SparseCore 0:
  11.1 154.1 all-gather.1
  202.4 28.6 reduce-scatter.1
where the time goes:
time: 262 us; the launch traced here: 261 us
  waiting for transfers between devices  164 us (63%)
  starting transfers between devices  33.3 us (13%)
  blocking collectives  20.9 us (8%)
  between operations  14.2 us (5%)
  local copies, waits for them, and re-layouts  12.6 us (5%)
  matrix products  9.07 us (3%)
  other arithmetic  6.63 us (3%)
    all_gather x1, waiting for transfers between devices, per_device(): lax.all_gather(kv_weight, ('sec', 'seq'), axis=0, tiled=True)  72.2 us
    all_to_all x1, waiting for transfers between devices, per_device(): lax.all_to_all(send_rows, ('sec', 'seq'), split_axis=0, concat_axis=0, ti...  43.4 us
    reduce_scatter x1, waiting for transfers between devices, per_device(): lax.psum_scatter(partial_value, 'tp', scatter_dimension=1, tiled=True)  28.7 us
    all_to_all x1, starting transfers between devices, per_device(): lax.all_to_all(send_rows, ('sec', 'seq'), split_axis=0, concat_axis=0, ti...  20.4 us
    all_to_all x1, waiting for transfers between devices, per_device(): lax.all_to_all(back_rows, ('sec', 'seq'), split_axis=0, concat_axis=0, ti...  19.4 us
    all_to_all x1, starting transfers between devices, per_device(): lax.all_to_all(back_rows, ('sec', 'seq'), split_axis=0, concat_axis=0, ti...  12.8 us
    all_gather x1, blocking collectives, per_device(): cot_all = lax.all_gather(kv_cot, 'tp', axis=1, tiled=True)  12.5 us
    psum x1, blocking collectives, per_device(): sumsq = lax.psum(jnp.sum(hidden * hidden, axis=1), 'tp')  8.46 us
  transfers between devices with their start and end apart: 4, of which 4 were waited for; matrix products, arithmetic and copies ran while one was open for 5% of the time, Pallas kernels for 0%

commit v1 on v0

v1 whole, which is shorter than its diff:
```python
import jax
import jax.numpy as jnp
from jax import lax
from jax.sharding import PartitionSpec as P

D = 8192
EPS = 1e-06


def pair_position(owner):
    n = owner.shape[0]
    order = jnp.arange(n, dtype=jnp.int32)
    same = (owner[:, None] == owner[None, :]) & (order[:, None] < order[None, :])
    rank = jnp.sum(same.astype(jnp.int32), axis=0)
    return jnp.where(owner >= 0, 2 * owner + rank, -1)


def per_device(text_embed, image_rows, token_source, slot_dest, norm_gain, kv_weight, kv_cot):
    tok = text_embed.shape[0]
    slots = image_rows.shape[0]
    axes = ("sec", "seq")
    peers = lax.axis_size("sec") * lax.axis_size("seq")
    place = jnp.arange(2 * peers, dtype=jnp.int32)
    is_image = token_source >= 0
    filled = slot_dest >= 0
    pos_tok = pair_position(jnp.where(is_image, token_source // slots, -1))
    pos_slot = pair_position(jnp.where(filled, slot_dest // tok, -1))
    pick_tok = (place[:, None] == pos_tok[None, :]).astype(jnp.bfloat16)
    pick_slot = (place[:, None] == pos_slot[None, :]).astype(jnp.bfloat16)

    def move(pick_send, pick_recv, rows):
        send = jnp.dot(pick_send, rows, preferred_element_type=jnp.float32).astype(jnp.bfloat16)
        got = lax.all_to_all(send, axes, split_axis=0, concat_axis=0, tiled=True)
        return lax.dot_general(
            pick_recv, got, (((0,), (0,)), ((), ())), preferred_element_type=jnp.float32
        ).astype(jnp.bfloat16)

    cot_img = move(pick_tok, pick_slot, kv_cot)
    cot = lax.all_gather(jnp.concatenate([kv_cot, cot_img]), "tp", axis=1, tiled=True)
    weight = lax.all_gather(kv_weight, axes, axis=0, tiled=True)
    rows = jnp.concatenate([text_embed, image_rows]).astype(jnp.float32)
    gained = (rows * norm_gain).astype(jnp.bfloat16)
    partial = lax.dot_general(
        gained, weight, (((1,), (1,)), ((), ())), preferred_element_type=jnp.float32
    )
    sums = jnp.stack([jnp.sum(rows * rows, axis=1), jnp.sum(partial * cot.astype(jnp.float32), axis=1)])
    sumsq, dots = lax.psum(sums, "tp")
    scale = lax.rsqrt(sumsq / D + EPS)
    raw = lax.psum_scatter(partial, "tp", scatter_dimension=1, tiled=True)
    kv = (raw * scale[:, None]).astype(jnp.bfloat16)
    kv_img = move(pick_slot, pick_tok, kv[tok:])
    key_value = jnp.where(is_image[:, None], kv_img, kv[:tok])
    normed_grad = jnp.dot(cot, weight, preferred_element_type=jnp.float32)
    grad = scale[:, None] * (norm_gain * normed_grad) - rows * (scale * scale * scale * dots / D)[:, None]
    grad = grad.astype(jnp.bfloat16)
    text_grad = jnp.where(is_image[:, None], jnp.zeros_like(grad[:tok]), grad[:tok])
    image_grads = jnp.where(filled[:, None], grad[tok:], jnp.zeros_like(grad[tok:]))
    return key_value, text_grad, image_grads


def solution(mesh):
    both = P(("sec", "seq"), "tp")
    rows = P(("sec", "seq"))
    return jax.shard_map(
        per_device,
        mesh=mesh,
        in_specs=(both, both, rows, rows, P("tp"), both, both),
        out_specs=(both, both, both),
        check_vma=False,
    )
```

time: 262 us -> 238 us (0.908)
  waiting for transfers between devices: 164 us -> 144 us
  local copies, waits for them, and re-layouts: 12.6 us -> 1.81 us
  starting transfers between devices: 33.3 us -> 38 us
  matrix products: 9.07 us -> 12.3 us
    all_to_all x2, waiting for transfers between devices: 62.8 us -> 31.4 us  [move(): got = lax.all_to_all(send, axes, split_axis=0, concat_axis=0, tiled=True)]
    all_gather x1, waiting for transfers between devices: 72.2 us -> 97.1 us  [per_device(): weight = lax.all_gather(kv_weight, axes, axis=0, tiled=True)]
    reduce_scatter x1, waiting for transfers between devices: 28.7 us -> 14.7 us  [per_device(): raw = lax.psum_scatter(partial, 'tp', scatter_dimension=1, tiled=True)]
    scatter x2 -> x0, local copies, waits for them, and re-layouts: 5.29 us -> none  [the longest x1 3.08 us: per_device(): jnp.zeros((buffer_rows, feat_count), jnp.bfloat16).at[back_pos]]
    all_to_all x2, starting transfers between devices: 33.2 us -> 37.9 us  [move(): got = lax.all_to_all(send, axes, split_axis=0, concat_axis=0, tiled=True)]
    gather x2 -> x0, local copies, waits for them, and re-layouts: 3.26 us -> none  [the longest x1 2.33 us: per_device(): picked = jnp.take(received, take_pos, axis=0)]
    dot_general x2 -> x6, matrix products: 9.07 us -> 12.3 us  [the longest x1 5.7 us: per_device(): lax.dot_general(gained, weight, (((1,), (1,)), ((), ())), preferred_eleme...]
where the time goes in v1:
time: 238 us
  waiting for transfers between devices  144 us (61%)
  starting transfers between devices  38 us (16%)
  blocking collectives  19.9 us (8%)
  between operations  14.1 us (6%)
  matrix products  12.3 us (5%)
  other arithmetic  7.43 us (3%)
    all_gather x1, waiting for transfers between devices, per_device(): weight = lax.all_gather(kv_weight, axes, axis=0, tiled=True)  97.1 us
    all_to_all x2, starting transfers between devices, move(): got = lax.all_to_all(send, axes, split_axis=0, concat_axis=0, tiled=True)  37.9 us
    all_to_all x2, waiting for transfers between devices, move(): got = lax.all_to_all(send, axes, split_axis=0, concat_axis=0, tiled=True)  31.4 us
    reduce_scatter x1, waiting for transfers between devices, per_device(): raw = lax.psum_scatter(partial, 'tp', scatter_dimension=1, tiled=True)  14.7 us
    all_gather x1, blocking collectives, per_device(): lax.all_gather(jnp.concatenate([kv_cot, cot_img]), 'tp', axis=1, tiled=True)  11.4 us
    psum x1, blocking collectives, per_device(): sumsq, dots = lax.psum(sums, 'tp')  8.46 us
    dot_general x1, matrix products, per_device(): lax.dot_general(gained, weight, (((1,), (1,)), ((), ())), preferred_eleme...  5.7 us
  transfers between devices with their start and end apart: 4, of which 4 were waited for; matrix products, arithmetic and copies ran while one was open for 5% of the time, Pallas kernels for 0%

profile of v1, /device:TPU:1, one launch (start us, length us, event | category | flops | bytes accessed | tf_op | source)
XLA Modules:
  0.0 237.6 jit_solution(10239485853748250789)
XLA Ops:
  7.2 0.7 all-gather.2.cloned.1.call-update
  7.9 0.7 fusion.20
  8.7 0.7 compare_select_fusion.1
  9.4 1.1 convolution_convert_fusion.1
  10.5 0.7 all_to_all.16
  11.2 20.4 %all-to-all-start = ((bf16[128,2,256]{2,1,0:T(2,128)(2,1)}), bf16[128,2,256]{2,1,0:T(2,128)(2,1)S(1)}, u32[]{:S(2)}, u32[]{:S(2)}) async-start(bf16[128,2,256]{2,1,0:T(2,128)(2,1)} %all_to_all.16), calls=%async_computation.1 | async-start | bytes 262144 | tf_op jit(solution)/shard_map/all_to_all | solution.py:33
  31.7 0.7 fusion.21
  32.4 0.7 compare_select_fusion
  33.1 16.0 %all-to-all-done = bf16[128,2,256]{2,1,0:T(2,128)(2,1)S(1)} async-done(((bf16[128,2,256]{2,1,0:T(2,128)(2,1)}), bf16[128,2,256]{2,1,0:T(2,128)(2,1)S(1)}, u32[]{:S(2)}, u32[]{:S(2)}) %all-to-all-start) | async-done | bytes 131104 | tf_op jit(solution)/shard_map/all_to_all | solution.py:33
  49.4 0.9 pad_maximum_fusion.2
  50.3 11.4 %all_gather.7 = bf16[384,1024]{1,0:T(8,128)(2,1)S(1)} all-gather(bf16[384,256]{1,0:T(8,128)(2,1)S(1)} %pad_maximum_fusion.2), channel_id=1, replica_groups=mesh['sec'=4,'seq'=32,'tp'=4] {'tp'}, dimensions={1}, use_global_device_ids=true | all-gather | bytes 983040 | tf_op jit(solution)/shard_map/all_gather | solution.py:39
  61.8 97.1 %all-gather.2.cloned.1.call-done = bf16[1024,2048]{1,0:T(8,128)(2,1)} async-done(((bf16[8,2048]{1,0:T(8,128)(2,1)}), bf16[1024,2048]{1,0:T(8,128)(2,1)}) %all-gather.2.cloned.1.call-update) | async-done | bytes 4194320 | tf_op jit(solution)/shard_map/all_gather | solution.py:40
  158.9 5.7 %multiply_reduce_fusion = (f32[384]{0:T(512)S(1)}, f32[384,1024]{1,0:T(8,128)}) fusion(bf16[384,1024]{1,0:T(8,128)(2,1)S(1)} %all_gather.7, bf16[1024,2048]{1,0:T(8,128)(2,1)} %all-gather.2.cloned.1.call-done, f32[2048]{0:T(1024)} %param.11, bf16[128,2048]{1,0:T(8,128)(2,1)} %param.8, bf16[256,2048]{1,0:T(8,128)(2,1)} %param.7), kind=kOutput, calls=%fused_computation.9 | convolution fusion | flops 1616510592 | bytes 8136192 | tf_op jit(solution)/shard_map/dot_general | solution.py:43
  164.7 0.4 fusion.1
  165.3 8.5 %psum.7 = f32[2,384]{1,0:T(2,128)S(1)} all-reduce(f32[2,384]{1,0:T(2,128)S(1)} %pad_maximum_fusion.3), channel_id=1, replica_groups=mesh['sec'=4,'seq'=32,'tp'=4] {'tp'}, use_global_device_ids=true, to_apply=%region_5.6 | all-reduce | flops 768 | bytes 6144 | tf_op jit(solution)/shard_map/psum | solution.py:47
  173.8 4.2 %fusion.3 = bf16[384,2048]{1,0:T(8,128)(2,1)S(1)} fusion(bf16[384,1024]{1,0:T(8,128)(2,1)S(1)} %all_gather.7, bf16[1024,2048]{1,0:T(8,128)(2,1)} %all-gather.2.cloned.1.call-done, f32[384]{0:T(512)S(1)} %fusion.16, f32[384]{0:T(512)S(1)} %get-tuple-element.4, f32[2048]{0:T(1024)S(1)} %copy-done.3, bf16[128,2048]{1,0:T(8,128)(2,1)} %param.8, ...), kind=kOutput, calls=%fused_computation.6 | convolution fusion | flops 1617690624 | bytes 8137728 | tf_op jit(solution)/shard_map/dot_general | solution.py:53
  178.1 14.7 %reduce-scatter.2.cloned.1.call-done = f32[384,256]{1,0:T(8,128)} async-done(((f32[384,1024]{1,0:T(8,128)}), f32[384,256]{1,0:T(8,128)}) %reduce-scatter.2.cloned.1.call-update) | async-done | bytes 393232 | tf_op jit(solution)/shard_map/reduce_scatter | solution.py:49
  192.8 1.1 multiply_convert_fusion
  194.1 0.7 all_to_all.19
  194.8 17.5 %all-to-all-start.1 = ((bf16[128,2,256]{2,1,0:T(2,128)(2,1)}), bf16[128,2,256]{2,1,0:T(2,128)(2,1)S(1)}, u32[]{:S(2)}, u32[]{:S(2)}) async-start(bf16[128,2,256]{2,1,0:T(2,128)(2,1)} %all_to_all.19), calls=%async_computation.2 | async-start | bytes 262144 | tf_op jit(solution)/shard_map/all_to_all | solution.py:33
  212.3 0.9 slice_select_fusion.1
  213.2 1.1 slice_select_fusion
  214.3 15.4 %all-to-all-done.1 = bf16[128,2,256]{2,1,0:T(2,128)(2,1)S(1)} async-done(((bf16[128,2,256]{2,1,0:T(2,128)(2,1)}), bf16[128,2,256]{2,1,0:T(2,128)(2,1)S(1)}, u32[]{:S(2)}, u32[]{:S(2)}) %all-to-all-start.1) | async-done | bytes 131104 | tf_op jit(solution)/shard_map/all_to_all | solution.py:33
  229.8 0.9 fusion.7
  (26 shorter events, 1.1 us)
Async XLA Ops:
  7.2 151.8 %all-gather.2.cloned.1.call-start = ((), (), s32[]{:S(2)}) async-start(), calls=%async_computation.3 | async-start | bytes 4227072 | tf_op jit(solution)/shard_map/all_gather | solution.py:40
  11.2 37.9 %all-to-all-start = ((bf16[128,2,256]{2,1,0:T(2,128)(2,1)}), bf16[128,2,256]{2,1,0:T(2,128)(2,1)S(1)}, u32[]{:S(2)}, u32[]{:S(2)}) async-start(bf16[128,2,256]{2,1,0:T(2,128)(2,1)} %all_to_all.16), calls=%async_computation.1 | async-start | bytes 262144 | tf_op jit(solution)/shard_map/all_to_all | solution.py:33
  31.6 161.2 %reduce-scatter.2.cloned.1.call-start = ((), (), s32[]{:S(2)}) async-start(), calls=%async_computation.4 | async-start | bytes 1966080 | tf_op jit(solution)/shard_map/reduce_scatter | solution.py:49
  61.8 102.9 %copy-start = (bf16[256,2048]{1,0:T(8,128)(2,1)S(1)}, bf16[256,2048]{1,0:T(8,128)(2,1)}, u32[]{:S(2)}) copy-start(bf16[256,2048]{1,0:T(8,128)(2,1)} %param.7) | copy-start | bytes 3145732
  61.8 102.9 %copy-start.1 = (bf16[128,2048]{1,0:T(8,128)(2,1)S(1)}, bf16[128,2048]{1,0:T(8,128)(2,1)}, u32[]{:S(2)}) copy-start(bf16[128,2048]{1,0:T(8,128)(2,1)} %param.8) | copy-start | bytes 1572868
  164.6 0.7 copy-start.4
  164.6 0.7 copy-start.2
  164.6 9.2 %copy-start.3 = (f32[2048]{0:T(1024)S(1)}, f32[2048]{0:T(1024)}, u32[]{:S(2)}) copy-start(f32[2048]{0:T(1024)} %param.11) | copy-start | bytes 24580
  194.8 34.9 %all-to-all-start.1 = ((bf16[128,2,256]{2,1,0:T(2,128)(2,1)}), bf16[128,2,256]{2,1,0:T(2,128)(2,1)S(1)}, u32[]{:S(2)}, u32[]{:S(2)}) async-start(bf16[128,2,256]{2,1,0:T(2,128)(2,1)} %all_to_all.19), calls=%async_computation.2 | async-start | bytes 262144 | tf_op jit(solution)/shard_map/all_to_all | solution.py:33
Sparse Core Ops, SparseCore 0:
  11.1 147.7 all-gather.1
  164.8 27.9 reduce-scatter.1

commit v2 on v1

v2 whole, which is shorter than its diff:
```python
import functools

import jax
import jax.numpy as jnp
from jax import lax
from jax.experimental import pallas as pl
from jax.experimental.pallas import tpu as pltpu
from jax.sharding import PartitionSpec as P

D = 8192
EPS = 1e-06
F32 = jnp.float32
BF16 = jnp.bfloat16
MESH = pl.DeviceIdType.MESH
LANES = 128


class Pair:
    def __init__(self, out, into):
        self.ends = (out, into)

    def __getitem__(self, i):
        return self.ends[i]()


def shift_of(n):
    return n.bit_length() - 1


def places(row, log_owner, nx, nseq):
    n = row.shape[1]
    own = lax.shift_right_arithmetic(row, jnp.full_like(row, log_owner))
    own_row = own.astype(F32)
    ii = lax.broadcasted_iota(jnp.int32, (n, n), 0)
    jj = lax.broadcasted_iota(jnp.int32, (n, n), 1)
    own_col = jnp.sum(jnp.where(ii == jj, own_row, 0.0), axis=1, keepdims=True)
    eq = own_col == own_row
    rank_row = jnp.sum(jnp.where(eq & (ii < jj), 1.0, 0.0), axis=0, keepdims=True)
    rank_col = jnp.sum(jnp.where(eq & (jj < ii), 1.0, 0.0), axis=1, keepdims=True)
    x_of = lax.shift_right_arithmetic(own, jnp.full_like(own, shift_of(nseq)))
    s_of = own & (nseq - 1)
    key = ((s_of * nx + x_of) * 2).astype(F32) + rank_row
    key = jnp.where(own_row >= 0.0, key, -1.0)
    pos = jnp.where(own_col >= 0.0, own_col * 2.0 + rank_col, -1.0)
    return key, pos, own_col


def kernel(
    nx, nz, ny,
    text, img, ts, sd, gain, w, cot,
    kv_out, tg_out, ig_out,
    wsend, wsib, wq, xg, cots, sq, acc, kvp, rs_send, rs_recv, sum_send, sum_recv,
    b1a, r1a, b2a, r2a, b1b, r1b, b2b, r2b,
    sib_sem, ax_s, ax_r, z_s, z_r, bx_s, bx_r, sa_s, sa_r, sb_s, sb_r,
    e1_s, e1_r, e2_s, e2_r, yc_s, yc_r, rs_s, rs_r, sm_s, sm_r,
):
    x, s, y = lax.axis_index("sec"), lax.axis_index("seq"), lax.axis_index("tp")
    z, c = s // 2, s % 2
    nseq = 2 * nz
    tok, feat = text.shape
    slots = img.shape[0]
    rows = tok + slots
    cols = cot.shape[1]
    halves = cols // LANES
    npos = 2 * nx * nseq
    fq = feat // 4
    nr, nl = nz // 2, (nz - 1) // 2

    def remote(src, dst, ss, rs, dev):
        return pltpu.make_async_remote_copy(
            src_ref=src, dst_ref=dst, send_sem=ss, recv_sem=rs, device_id=dev, device_id_type=MESH
        )

    def loop(lo, hi, body):
        if hi > lo:
            lax.fori_loop(lo, hi, lambda i, t: (body(i), t)[1], 0)

    barrier = pltpu.get_barrier_semaphore()

    def greet(dev):
        pl.semaphore_signal(barrier, inc=1, device_id=dev, device_id_type=MESH)

    loop(1, nseq, lambda k: greet((x, lax.rem(s + k, nseq), y)))
    for k in range(1, nx):
        greet((lax.rem(x + k, nx), s, y))
    for k in range(1, ny):
        greet((x, s, lax.rem(y + k, ny)))

    half = feat // 2
    w8 = w[...].astype(F32)
    wsend[...] = jnp.concatenate([w8[:, :half], w8[:, half:]], axis=0).astype(BF16)
    key_tok, pos_tok, own_tok = places(ts[...], shift_of(slots), nx, nseq)
    key_slot, pos_slot, own_slot = places(sd[...], shift_of(tok), nx, nseq)

    def pick_rows(key):
        n = key.shape[1]
        return jnp.where(lax.broadcasted_iota(jnp.int32, (npos, n), 0).astype(F32) == key, 1.0, 0.0).astype(BF16)

    def pick_cols(pos):
        n = pos.shape[0]
        return jnp.where(lax.broadcasted_iota(jnp.int32, (n, npos), 1).astype(F32) == pos, 1.0, 0.0).astype(BF16)

    def fill1(key, values, b1, r1):
        g = jnp.dot(pick_rows(key), values, preferred_element_type=F32)
        parts = [g[:, h * LANES : (h + 1) * LANES].reshape(nseq, 2 * nx, LANES) for h in range(halves)]
        b1[...] = jnp.concatenate(parts, axis=1).astype(BF16)
        r1[s] = b1[s]

    def fill2(r1, b2, r2):
        r = r1[...].astype(F32)
        m = jnp.concatenate(
            [r[:, h * 2 * nx : (h + 1) * 2 * nx].reshape(npos, LANES) for h in range(halves)], axis=1
        ).astype(BF16)
        i = lax.broadcasted_iota(jnp.int32, (npos, npos), 0)
        j = lax.broadcasted_iota(jnp.int32, (npos, npos), 1)
        lx, ls = shift_of(2 * nseq), shift_of(nseq)
        i_x = lax.shift_right_arithmetic(i, jnp.full_like(i, lx))
        i_s = lax.shift_right_arithmetic(i, jnp.full_like(i, 1)) & (nseq - 1)
        perm = jnp.where((i_s * nx + i_x) * 2 + (i & 1) == j, 1.0, 0.0).astype(BF16)
        b2[...] = jnp.dot(perm, m, preferred_element_type=F32).astype(BF16).reshape(nx, 2 * nseq, cols)
        r2[x] = b2[x]

    def take(pos, r2):
        return jnp.dot(pick_cols(pos), r2[...].reshape(npos, cols), preferred_element_type=F32)

    def copy1(n, b1, r1, k):
        to, frm = lax.rem(s + k, nseq), lax.rem(s + nseq - k, nseq)
        return Pair(
            lambda: remote(b1.at[to], r1.at[s], e1_s.at[n, k], e1_r.at[n, k], (x, to, y)),
            lambda: remote(b1.at[to], r1.at[frm], e1_s.at[n, k], e1_r.at[n, k], (x, to, y)),
        )

    def copy2(n, b2, r2, k):
        to, frm = lax.rem(x + k, nx), lax.rem(x + nx - k, nx)
        return Pair(
            lambda: remote(b2.at[to], r2.at[x], e2_s.at[n, k], e2_r.at[n, k], (to, s, y)),
            lambda: remote(b2.at[to], r2.at[frm], e2_s.at[n, k], e2_r.at[n, k], (to, s, y)),
        )

    fill1(key_tok, cot[...], b1a, r1a)
    cots[y, :tok] = cot[...]

    pl.semaphore_wait(barrier, nseq - 1 + nx - 1 + ny - 1)

    sib = (x, s + 1 - 2 * c, y)
    swap = remote(wsend, wsib, sib_sem.at[0], sib_sem.at[1], sib)
    swap.start()
    loop(1, nseq, lambda k: copy1(0, b1a, r1a, k)[0].start())

    def copy_y(part, k):
        to, frm = lax.rem(y + k, ny), lax.rem(y + ny - k, ny)
        n = tok if part == 0 else slots
        lo = 0 if part == 0 else tok
        return Pair(
            lambda: remote(cots.at[y, pl.ds(lo, n)], cots.at[y, pl.ds(lo, n)], yc_s.at[part, k], yc_r.at[part, k], (x, s, to)),
            lambda: remote(cots.at[y, pl.ds(lo, n)], cots.at[frm, pl.ds(lo, n)], yc_s.at[part, k], yc_r.at[part, k], (x, s, to)),
        )

    for k in range(1, ny):
        copy_y(0, k)[0].start()

    swap.wait()
    first = c == 0
    mine = jnp.where(first, wsend[0:8].astype(F32), wsend[8:16].astype(F32))
    other = jnp.where(first, wsib[0:8].astype(F32), wsib[8:16].astype(F32))
    piece = jnp.concatenate([jnp.where(first, mine, other), jnp.where(first, other, mine)], axis=0).astype(BF16)
    qa, qb = 2 * c, 2 * c + 1
    wq[qa, x, z] = piece[:, :fq]
    wq[qb, x, z] = piece[:, fq:]

    def copy_ax(k):
        to, frm = lax.rem(x + k, nx), lax.rem(x + nx - k, nx)
        return Pair(
            lambda: remote(wq.at[qa, x, z], wq.at[qa, x, z], ax_s.at[k], ax_r.at[k], (to, s, y)),
            lambda: remote(wq.at[qa, x, z], wq.at[qa, frm, z], ax_s.at[k], ax_r.at[k], (to, s, y)),
        )

    def origin(d, k):
        return lax.rem(z + nz - k, nz) if d == 0 else lax.rem(z + k, nz)

    def block(b, o):
        return wq.at[qb, x, o] if b else wq.at[qa, :, o]

    def copy_z(b, d, k):
        to = lax.rem(z + 1, nz) if d == 0 else lax.rem(z + nz - 1, nz)
        out, into = block(b, origin(d, k - 1)), block(b, origin(d, k))
        dev = (x, 2 * to + c, y)
        return Pair(
            lambda: remote(out, out, z_s.at[b, d, k], z_r.at[b, d, k], dev),
            lambda: remote(into, into, z_s.at[b, d, k], z_r.at[b, d, k], dev),
        )

    def copy_bx(o, j, k):
        to, frm = lax.rem(x + k, nx), lax.rem(x + nx - k, nx)
        return Pair(
            lambda: remote(wq.at[qb, x, o], wq.at[qb, x, o], bx_s.at[j, k], bx_r.at[j, k], (to, s, y)),
            lambda: remote(wq.at[qb, x, o], wq.at[qb, frm, o], bx_s.at[j, k], bx_r.at[j, k], (to, s, y)),
        )

    def copy_sib(b, o, j):
        q, other_q = (qb, 3 - qa) if b else (qa, 2 - qa)
        ss, rr = (sb_s, sb_r) if b else (sa_s, sa_r)
        return Pair(
            lambda: remote(wq.at[q, :, o], wq.at[q, :, o], ss.at[j], rr.at[j], sib),
            lambda: remote(wq.at[q, :, o], wq.at[other_q, :, o], ss.at[j], rr.at[j], sib),
        )

    for k in range(1, nx):
        copy_ax(k)[0].start()
    copy_z(1, 0, 1)[0].start()
    if nl:
        copy_z(1, 1, 1)[0].start()
    for k in range(1, nx):
        copy_bx(z, 0, k)[0].start()

    def prepare(ref, base):
        def body(i):
            r = ref[pl.ds(pl.multiple_of(i * 16, 16), 16), :].astype(F32)
            at = pl.ds(pl.multiple_of(base + i * 16, 16), 16)
            xg[at, :] = (r * gain[...]).astype(BF16)
            sq[at, :] = jnp.broadcast_to(jnp.sum(r * r, axis=1, keepdims=True), (16, LANES))

        loop(0, ref.shape[0] // 16, body)

    for k in range(1, nx):
        copy_ax(k)[1].wait_recv()
    copy_z(0, 0, 1)[0].start()
    if nl:
        copy_z(0, 1, 1)[0].start()
    copy_sib(0, z, 0)[0].start()

    prepare(text, 0)

    def finish_b(o, j):
        for k in range(1, nx):
            copy_bx(o, j, k)[1].wait_recv()
        copy_sib(1, o, j)[0].start()

    def arrive(b, d, k):
        n = nr if d == 0 else nl
        o, j = origin(d, k), 2 * k - 1 + d
        copy_z(b, d, k)[1].wait_recv()

        @pl.when(k < n)
        def _():
            copy_z(b, d, k + 1)[0].start()

        if b:
            for i in range(1, nx):
                copy_bx(o, j, i)[0].start()
        else:
            copy_sib(0, o, j)[0].start()

    def ring(k):
        for b in (1, 0):
            arrive(b, 0, k)

            @pl.when(k <= nl)
            def _():
                arrive(b, 1, k)

        @pl.when(k == 1)
        def _():
            finish_b(z, 0)

        @pl.when(k > 1)
        def _():
            finish_b(origin(0, k - 1), 2 * k - 3)
            finish_b(origin(1, k - 1), 2 * k - 2)

    cut1, cut2 = max(nr // 4, 1), max(nr // 2, 1)
    loop(1, cut1 + 1, ring)
    prepare(img, tok)
    loop(1, nseq, lambda k: copy1(0, b1a, r1a, k)[1].wait_recv())
    fill2(r1a, b2a, r2a)
    for k in range(1, nx):
        copy2(0, b2a, r2a, k)[0].start()
    loop(cut1 + 1, cut2 + 1, ring)
    for k in range(1, nx):
        copy2(0, b2a, r2a, k)[1].wait_recv()
    cots[y, tok:] = take(pos_slot, r2a).astype(BF16)
    for k in range(1, ny):
        copy_y(1, k)[0].start()
    loop(cut2 + 1, nr + 1, ring)
    finish_b(origin(0, nr), 2 * nr - 1)
    if nl == nr:
        finish_b(origin(1, nr), 2 * nr)
    for part in range(2):
        for k in range(1, ny):
            copy_y(part, k)[1].wait_recv()
    for b in range(2):
        copy_sib(b, z, 0)[1].wait_recv()
        loop(1, nr + 1, lambda k, b=b: copy_sib(b, origin(0, k), 2 * k - 1)[1].wait_recv())
        loop(1, nl + 1, lambda k, b=b: copy_sib(b, origin(1, k), 2 * k)[1].wait_recv())

    def copy_rs(k):
        to = lax.rem(y + k, ny)
        return remote(rs_send.at[k], rs_recv.at[k], rs_s.at[k], rs_r.at[k], (x, s, to))

    def copy_sum(k):
        to = lax.rem(y + k, ny)
        return remote(sum_send, sum_recv.at[k], sm_s.at[k], sm_r.at[k], (x, s, to))

    dots = jnp.zeros((rows, 1), F32)
    for k in list(range(1, ny)) + [0]:
        t = lax.rem(y + k, ny)
        part = jnp.zeros((rows, cols), F32)
        for q in range(4):
            part = part + lax.dot_general(
                xg[:, q * fq : (q + 1) * fq],
                wq[q, t].reshape(16 * nz, fq),
                (((1,), (1,)), ((), ())),
                preferred_element_type=F32,
            )
        if k:
            rs_send[k] = part.astype(BF16)
            copy_rs(k).start()
        else:
            kvp[...] = part
        dots = dots + jnp.sum(part * cots[t].astype(F32), axis=1, keepdims=True)
    lane = lax.broadcasted_iota(jnp.int32, (rows, LANES), 1)
    both = jnp.where(lane == 0, sq[...], jnp.where(lane == 1, dots, 0.0))
    sum_send[...] = jnp.transpose(both)[:8]
    for k in range(1, ny):
        copy_sum(k).start()

    cot_all = jnp.concatenate([cots[t] for t in range(ny)], axis=1)
    for q in range(4):
        acc[:, q * fq : (q + 1) * fq] = jnp.dot(
            cot_all, wq[q].reshape(nx * nz * 16, fq), preferred_element_type=F32
        )

    total = sum_send[...]
    for k in range(1, ny):
        copy_sum(k).wait_recv()
        total = total + sum_recv[k]
    scale_r = lax.rsqrt(total[0:1] / D + EPS)
    coef_r = scale_r * scale_r * scale_r * total[1:2] / D
    flat = jnp.concatenate([scale_r, coef_r, jnp.zeros((LANES - 2, rows), F32)], axis=0)
    sq[...] = jnp.transpose(flat)
    scale = sq[:, 0:1]

    raw = kvp[...]
    for k in range(1, ny):
        copy_rs(k).wait_recv()
        raw = raw + rs_recv[k].astype(F32)
    kv = raw * scale
    kvp[...] = kv
    fill1(key_slot, kv[tok:].astype(BF16), b1b, r1b)
    loop(1, nseq, lambda k: copy1(1, b1b, r1b, k)[0].start())

    keep = jnp.concatenate(
        [jnp.where(own_tok < 0.0, 1.0, 0.0), jnp.where(own_slot >= 0.0, 1.0, 0.0)], axis=0
    )
    sq[...] = jnp.where(lane == 2, keep, sq[...])

    def body_of(ref, base, out):
        def body(i):
            here = pl.ds(pl.multiple_of(i * 16, 16), 16)
            at = pl.ds(pl.multiple_of(base + i * 16, 16), 16)
            r = ref[here, :].astype(F32)
            f = sq[at, :]
            g = f[:, 0:1] * (gain[...] * acc[at, :]) - r * f[:, 1:2]
            out[here, :] = jnp.where(f[:, 2:3] > 0.0, g, 0.0).astype(BF16)

        loop(0, ref.shape[0] // 16, body)

    body_of(text, 0, tg_out)
    loop(1, nseq, lambda k: copy1(1, b1b, r1b, k)[1].wait_recv())
    fill2(r1b, b2b, r2b)
    for k in range(1, nx):
        copy2(1, b2b, r2b, k)[0].start()
    body_of(img, tok, ig_out)
    for k in range(1, nx):
        copy2(1, b2b, r2b, k)[1].wait_recv()
    got = take(pos_tok, r2b)
    kv_out[...] = jnp.where(own_tok >= 0.0, got, kvp[:tok]).astype(BF16)

    for k in range(1, nx):
        copy_ax(k)[0].wait_send()
        copy_bx(z, 0, k)[0].wait_send()
        copy2(0, b2a, r2a, k)[0].wait_send()
        copy2(1, b2b, r2b, k)[0].wait_send()
    for k in range(1, ny):
        copy_y(0, k)[0].wait_send()
        copy_y(1, k)[0].wait_send()
        copy_rs(k).wait_send()
        copy_sum(k).wait_send()

    def sent1(k):
        copy1(0, b1a, r1a, k)[0].wait_send()
        copy1(1, b1b, r1b, k)[0].wait_send()

    loop(1, nseq, sent1)
    for b in range(2):
        copy_sib(b, z, 0)[0].wait_send()
        for d, n in ((0, nr), (1, nl)):

            def sent(k, b=b, d=d):
                o, j = origin(d, k), 2 * k - 1 + d
                copy_z(b, d, k)[0].wait_send()
                copy_sib(b, o, j)[0].wait_send()
                if b:
                    for i in range(1, nx):
                        copy_bx(o, j, i)[0].wait_send()

            loop(1, n + 1, sent)


def per_device(text_embed, image_rows, token_source, slot_dest, norm_gain, kv_weight, kv_cot):
    nx, nseq, ny = lax.axis_size("sec"), lax.axis_size("seq"), lax.axis_size("tp")
    nz = nseq // 2
    tok, feat = text_embed.shape
    slots = image_rows.shape[0]
    rows = tok + slots
    cols = kv_cot.shape[1]
    nr = nz // 2
    dma = pltpu.SemaphoreType.DMA
    blk = (2 * nx * cols) // LANES
    exch = [
        pltpu.VMEM((nseq, blk, LANES), BF16),
        pltpu.VMEM((nseq, blk, LANES), BF16),
        pltpu.VMEM((nx, 2 * nseq, cols), BF16),
        pltpu.VMEM((nx, 2 * nseq, cols), BF16),
    ]
    vmem = pl.BlockSpec(memory_space=pltpu.VMEM)
    return pl.pallas_call(
        functools.partial(kernel, nx, nz, ny),
        out_shape=(
            jax.ShapeDtypeStruct((tok, cols), BF16),
            jax.ShapeDtypeStruct((tok, feat), BF16),
            jax.ShapeDtypeStruct((slots, feat), BF16),
        ),
        in_specs=[vmem] * 7,
        out_specs=(vmem, vmem, vmem),
        scratch_shapes=[
            pltpu.VMEM((16, feat // 2), BF16),
            pltpu.VMEM((16, feat // 2), BF16),
            pltpu.VMEM((4, nx, nz, 16, feat // 4), BF16),
            pltpu.VMEM((rows, feat), BF16),
            pltpu.VMEM((ny, rows, cols), BF16),
            pltpu.VMEM((rows, LANES), F32),
            pltpu.VMEM((rows, feat), F32),
            pltpu.VMEM((rows, cols), F32),
            pltpu.VMEM((ny, rows, cols), BF16),
            pltpu.VMEM((ny, rows, cols), BF16),
            pltpu.VMEM((8, rows), F32),
            pltpu.VMEM((ny, 8, rows), F32),
            *exch,
            *exch,
            dma((2,)),
            dma((nx,)),
            dma((nx,)),
            dma((2, 2, nr + 1)),
            dma((2, 2, nr + 1)),
            dma((nz, nx)),
            dma((nz, nx)),
            dma((nz,)),
            dma((nz,)),
            dma((nz,)),
            dma((nz,)),
            dma((2, nseq)),
            dma((2, nseq)),
            dma((2, nx)),
            dma((2, nx)),
            dma((2, ny)),
            dma((2, ny)),
            dma((ny,)),
            dma((ny,)),
            dma((ny,)),
            dma((ny,)),
        ],
        compiler_params=pltpu.CompilerParams(
            collective_id=0, has_side_effects=True, vmem_limit_bytes=50 * 2**20
        ),
        cost_estimate=pl.CostEstimate(
            flops=4 * rows * feat * cols * ny, bytes_accessed=8 * rows * feat, transcendentals=0
        ),
    )(
        text_embed,
        image_rows,
        token_source.reshape(1, tok),
        slot_dest.reshape(1, slots),
        norm_gain.reshape(1, feat),
        kv_weight,
        kv_cot,
    )


def solution(mesh):
    both = P(("sec", "seq"), "tp")
    rows = P(("sec", "seq"))
    return jax.shard_map(
        per_device,
        mesh=mesh,
        in_specs=(both, both, rows, rows, P("tp"), both, both),
        out_specs=(both, both, both),
        check_vma=False,
    )
```

time: 238 us -> 94.4 us (0.40)
  waiting for transfers between devices: 144 us -> 0 us
  Pallas kernels: 0 us -> 85.7 us
  starting transfers between devices: 38 us -> 0 us
  blocking collectives: 19.9 us -> 0 us
  between operations: 14.1 us -> 0.66 us
  matrix products: 12.3 us -> 0 us
  other arithmetic: 7.43 us -> 0 us
  local copies, waits for them, and re-layouts: 1.81 us -> 7.71 us
    all_gather x1 -> x0, waiting for transfers between devices: 97.1 us -> none  [per_device(): weight = lax.all_gather(kv_weight, axes, axis=0, tiled=True)]
    pallas_call x0 -> x1, Pallas kernels: none -> 85.7 us  [per_device(): pl.pallas_call(functools.partial(kernel, nx, nz, ny), out_shape=(jax.Shap...]
    all_to_all x2 -> x0, starting transfers between devices: 37.9 us -> none  [move(): got = lax.all_to_all(send, axes, split_axis=0, concat_axis=0, tiled=True)]
    all_to_all x2 -> x0, waiting for transfers between devices: 31.4 us -> none  [move(): got = lax.all_to_all(send, axes, split_axis=0, concat_axis=0, tiled=True)]
    reduce_scatter x1 -> x0, waiting for transfers between devices: 14.7 us -> none  [per_device(): raw = lax.psum_scatter(partial, 'tp', scatter_dimension=1, tiled=True)]
    dot_general x6 -> x0, matrix products: 12.3 us -> none  [the longest x1 5.7 us: per_device(): lax.dot_general(gained, weight, (((1,), (1,)), ((), ())), preferred_eleme...]
    all_gather x1 -> x0, blocking collectives: 11.4 us -> none  [per_device(): lax.all_gather(jnp.concatenate([kv_cot, cot_img]), 'tp', axis=1, tiled=True)]
    psum x1 -> x0, blocking collectives: 8.46 us -> none  [per_device(): sumsq, dots = lax.psum(sums, 'tp')]
  transfers between devices with their start and end apart: 4 -> 0, of which waited for: 4 -> 0; matrix products, arithmetic and copies ran while one was open for 5% -> 0% of each run, Pallas kernels for 0% -> 0%
where the time goes in v2:
time: 94.4 us; the launch traced here: 94.1 us
  Pallas kernels  85.7 us (91%)
  local copies, waits for them, and re-layouts  7.71 us (8%)
    pallas_call x1, Pallas kernels, per_device(): pl.pallas_call(functools.partial(kernel, nx, nz, ny), out_shape=(jax.Shap...  85.7 us
    unnamed x17, local copies, waits for them, and re-layouts  7.71 us

profile of v2, /device:TPU:1, one launch (start us, length us, event | category | flops | bytes accessed | tf_op | source)
XLA Modules:
  0.0 94.1 jit_solution(16326071283318562402)
XLA Ops:
  0.6 0.0 copy-start.5
  0.6 0.0 copy-start.6
  0.7 0.7 copy-done.5
  1.3 0.0 copy-done.6
  1.3 0.0 copy-start
  1.3 1.2 %copy-done = bf16[256,2048]{1,0:T(8,128)(2,1)S(1)} copy-done((bf16[256,2048]{1,0:T(8,128)(2,1)S(1)}, bf16[256,2048]{1,0:T(8,128)(2,1)}, u32[]{:S(2)}) %copy-start) | copy-done | bytes 1048600
  2.5 0.0 copy-start.1
  2.5 1.0 %copy-done.1 = bf16[128,2048]{1,0:T(8,128)(2,1)S(1)} copy-done((bf16[128,2048]{1,0:T(8,128)(2,1)S(1)}, bf16[128,2048]{1,0:T(8,128)(2,1)}, u32[]{:S(2)}) %copy-start.1) | copy-done | bytes 524312
  3.6 0.0 copy-start.2
  3.6 0.9 copy-done.2
  4.5 0.0 copy-start.3
  4.5 0.8 copy-done.3
  5.2 0.0 copy-start.4
  5.2 0.7 copy-done.4
  5.9 85.7 %shard_map.94 = (bf16[256,256]{1,0:T(8,128)(2,1)S(1)}, bf16[256,2048]{1,0:T(8,128)(2,1)S(1)}, bf16[128,2048]{1,0:T(8,128)(2,1)S(1)}) custom-call(bf16[256,2048]{1,0:T(8,128)(2,1)S(1)} %copy-done, bf16[128,2048]{1,0:T(8,128)(2,1)S(1)} %copy-done.1, s32[1,256]{1,0:T(1,128)S(1)} %bitcast.4, s32[1,128]{1,0:T(1,128)S(1)} %bitcast.5, f32[1,2048]{1,0:T(1,128)S(1)} %bitcast.3, ...), custom_call_target="tpu_custom_call" | custom-call | flops 3221225472 | bytes 6291456 | tf_op jit(solution)/shard_map/pallas_call | solution.py:427
  91.6 0.7 copy.13
  92.3 1.0 %copy.14 = bf16[256,2048]{1,0:T(8,128)(2,1)} copy(bf16[256,2048]{1,0:T(8,128)(2,1)S(1)} %get-tuple-element.7) | data formatting | bytes 2097152
  93.3 0.8 copy.15
Async XLA Ops:
  0.6 0.7 copy-start.5
  0.6 0.7 copy-start.6
  1.3 1.2 %copy-start = (bf16[256,2048]{1,0:T(8,128)(2,1)S(1)}, bf16[256,2048]{1,0:T(8,128)(2,1)}, u32[]{:S(2)}) copy-start(bf16[256,2048]{1,0:T(8,128)(2,1)} %text.1) | copy-start | bytes 3145732
  2.5 1.0 %copy-start.1 = (bf16[128,2048]{1,0:T(8,128)(2,1)S(1)}, bf16[128,2048]{1,0:T(8,128)(2,1)}, u32[]{:S(2)}) copy-start(bf16[128,2048]{1,0:T(8,128)(2,1)} %img.1) | copy-start | bytes 1572868
  3.6 0.9 copy-start.2
  4.5 0.8 copy-start.3
  5.2 0.7 copy-start.4

commit v3 on v1

v3 whole, which is shorter than its diff:
```python
import functools

import jax
import jax.numpy as jnp
from jax import lax
from jax.experimental import pallas as pl
from jax.experimental.pallas import tpu as pltpu
from jax.sharding import PartitionSpec as P

D = 8192
EPS = 1e-06
F32 = jnp.float32
BF16 = jnp.bfloat16
MESH = pl.DeviceIdType.MESH
LANES = 128


class Pair:
    def __init__(self, out, into):
        self.ends = (out, into)

    def __getitem__(self, i):
        return self.ends[i]()


def shift_of(n):
    return n.bit_length() - 1


def places(row, log_owner, nx, nseq):
    n = row.shape[1]
    own = lax.shift_right_arithmetic(row, jnp.full_like(row, log_owner))
    own_row = own.astype(F32)
    ii = lax.broadcasted_iota(jnp.int32, (n, n), 0)
    jj = lax.broadcasted_iota(jnp.int32, (n, n), 1)
    own_col = jnp.sum(jnp.where(ii == jj, own_row, 0.0), axis=1, keepdims=True)
    eq = own_col == own_row
    rank_row = jnp.sum(jnp.where(eq & (ii < jj), 1.0, 0.0), axis=0, keepdims=True)
    rank_col = jnp.sum(jnp.where(eq & (jj < ii), 1.0, 0.0), axis=1, keepdims=True)
    x_of = lax.shift_right_arithmetic(own, jnp.full_like(own, shift_of(nseq)))
    s_of = own & (nseq - 1)
    key = ((s_of * nx + x_of) * 2).astype(F32) + rank_row
    key = jnp.where(own_row >= 0.0, key, -1.0)
    pos = jnp.where(own_col >= 0.0, own_col * 2.0 + rank_col, -1.0)
    return key, pos, own_col


NEAR = (0, 3, -3, 6, -6)
ORDER = [(0, None)] + [(n, None) for n in NEAR[1:]] + [(n + e, (e, i)) for i, n in enumerate(NEAR) for e in (1, -1)] + [(8, None)]
LAG1, LAG2 = 3, 6
SLOT = {(n + 16) % 16: j for j, (n, _) in enumerate(ORDER)}


def kernel(
    nx, nz, ny,
    text_h, img_h, ts_h, sd_h, gain_h, w_h, cot_h,
    kv_out, tg_out, ig_out,
    text, img, ts, sd, gain, w, cot,
    wq, xg, cots, sq, acc, kvp, rs_send, rs_recv, sum_send, sum_recv,
    b1a, r1a, b2a, r2a, b1b, r1b, b2b, r2b,
    in_sem, z1_s, z1_r, z2_s, z2_r, z8_s, z8_r, x_s, x_r, sib_s, sib_r,
    e1_s, e1_r, e2_s, e2_r, yc_s, yc_r, rs_s, rs_r, sm_s, sm_r,
):
    x, s, y = lax.axis_index("sec"), lax.axis_index("seq"), lax.axis_index("tp")
    z, c = s // 2, s % 2
    nseq = 2 * nz
    tok, feat = text.shape
    slots = img.shape[0]
    rows = tok + slots
    cols = cot.shape[1]
    halves = cols // LANES
    npos = 2 * nx * nseq
    half = feat // 2

    def remote(src, dst, ss, rs, dev):
        return pltpu.make_async_remote_copy(
            src_ref=src, dst_ref=dst, send_sem=ss, recv_sem=rs, device_id=dev, device_id_type=MESH
        )

    def loop(lo, hi, body):
        if hi > lo:
            lax.fori_loop(lo, hi, lambda i, t: (body(i), t)[1], 0)

    pairs = [(w_h, w), (ts_h, ts), (cot_h, cot), (sd_h, sd), (gain_h, gain), (text_h, text), (img_h, img)]
    fetch = [pltpu.make_async_copy(p, q, in_sem.at[i]) for i, (p, q) in enumerate(pairs)]
    for f in fetch:
        f.start()

    barrier = pltpu.get_barrier_semaphore()

    def greet(dev):
        pl.semaphore_signal(barrier, inc=1, device_id=dev, device_id_type=MESH)

    loop(1, nseq, lambda k: greet((x, lax.rem(s + k, nseq), y)))
    for k in range(1, nx):
        greet((lax.rem(x + k, nx), s, y))
    for k in range(1, ny):
        greet((x, s, lax.rem(y + k, ny)))

    def at_z(o):
        return lax.rem(z + (o + nz) % nz, nz)

    def at_x(o):
        return lax.rem(x + (o + nx) % nx, nx)

    sib = (x, s + 1 - 2 * c, y)

    def copy_z1(i):
        n = NEAR[i]
        own, got = wq.at[x, 0, c], wq.at[x, i, c]
        dev = (x, 2 * at_z(-n) + c, y)
        return Pair(
            lambda: remote(own, got, z1_s.at[i], z1_r.at[i], dev),
            lambda: remote(got, got, z1_s.at[i], z1_r.at[i], dev),
        )

    def copy_z2(e, i):
        n, m = NEAR[i], (1 - e) // 2
        out, got = wq.at[x, i, c], wq.at[x, SLOT[(n + e) % 16], c]
        dev = (x, 2 * at_z(-e) + c, y)
        return Pair(
            lambda: remote(out, got, z2_s.at[m, i], z2_r.at[m, i], dev),
            lambda: remote(got, got, z2_s.at[m, i], z2_r.at[m, i], dev),
        )

    def copy_z8(m):
        n, to = (3, -2) if m == 0 else (4, 2)
        part = pl.ds(m * (half // 2), half // 2)
        out, got = wq.at[x, n, c, :, part], wq.at[x, SLOT[8], c, :, part]
        dev = (x, 2 * at_z(to) + c, y)
        return Pair(
            lambda: remote(out, got, z8_s.at[m], z8_r.at[m], dev),
            lambda: remote(got, got, z8_s.at[m], z8_r.at[m], dev),
        )

    def copy_x(j, m):
        up = m == 0 or (m == 2 and j % 2 == 0)
        frm = 0 if m < 2 else (-1 if up else 1)
        out = wq.at[at_x(frm), j, c]
        got = wq.at[at_x(frm + (-1 if up else 1)), j, c]
        dev = (at_x(1 if up else -1), s, y)
        return Pair(
            lambda: remote(out, out, x_s.at[j, m], x_r.at[j, m], dev),
            lambda: remote(got, got, x_s.at[j, m], x_r.at[j, m], dev),
        )

    def copy_sib(j):
        out, got = wq.at[:, j, c], wq.at[:, j, 1 - c]
        return Pair(
            lambda: remote(out, out, sib_s.at[j], sib_r.at[j], sib),
            lambda: remote(got, got, sib_s.at[j], sib_r.at[j], sib),
        )

    fetch[0].wait()
    w8 = w[...].astype(F32)
    wq[x, 0, c] = jnp.concatenate([w8[:, :half], w8[:, half:]], axis=0).astype(BF16)
    pl.semaphore_wait(barrier, nseq - 1 + nx - 1 + ny - 1)
    for i in range(1, 5):
        copy_z1(i)[0].start()
    copy_x(0, 0)[0].start()
    copy_x(0, 1)[0].start()
    copy_z2(1, 0)[0].start()
    copy_z2(-1, 0)[0].start()

    def pick_rows(key):
        n = key.shape[1]
        return jnp.where(lax.broadcasted_iota(jnp.int32, (npos, n), 0).astype(F32) == key, 1.0, 0.0).astype(BF16)

    def pick_cols(pos):
        n = pos.shape[0]
        return jnp.where(lax.broadcasted_iota(jnp.int32, (n, npos), 1).astype(F32) == pos, 1.0, 0.0).astype(BF16)

    def fill1(key, values, b1, r1):
        g = jnp.dot(pick_rows(key), values, preferred_element_type=F32)
        parts = [g[:, h * LANES : (h + 1) * LANES].reshape(nseq, 2 * nx, LANES) for h in range(halves)]
        b1[...] = jnp.concatenate(parts, axis=1).astype(BF16)
        r1[s] = b1[s]

    def fill2(r1, b2, r2):
        r = r1[...].astype(F32)
        m = jnp.concatenate(
            [r[:, h * 2 * nx : (h + 1) * 2 * nx].reshape(npos, LANES) for h in range(halves)], axis=1
        ).astype(BF16)
        i = lax.broadcasted_iota(jnp.int32, (npos, npos), 0)
        j = lax.broadcasted_iota(jnp.int32, (npos, npos), 1)
        lx, ls = shift_of(2 * nseq), shift_of(nseq)
        i_x = lax.shift_right_arithmetic(i, jnp.full_like(i, lx))
        i_s = lax.shift_right_arithmetic(i, jnp.full_like(i, 1)) & (nseq - 1)
        perm = jnp.where((i_s * nx + i_x) * 2 + (i & 1) == j, 1.0, 0.0).astype(BF16)
        b2[...] = jnp.dot(perm, m, preferred_element_type=F32).astype(BF16).reshape(nx, 2 * nseq, cols)
        r2[x] = b2[x]

    def take(pos, r2):
        return jnp.dot(pick_cols(pos), r2[...].reshape(npos, cols), preferred_element_type=F32)

    def copy1(n, b1, r1, k):
        to, frm = lax.rem(s + k, nseq), lax.rem(s + nseq - k, nseq)
        return Pair(
            lambda: remote(b1.at[to], r1.at[s], e1_s.at[n, k], e1_r.at[n, k], (x, to, y)),
            lambda: remote(b1.at[to], r1.at[frm], e1_s.at[n, k], e1_r.at[n, k], (x, to, y)),
        )

    def copy2(n, b2, r2, k):
        to, frm = lax.rem(x + k, nx), lax.rem(x + nx - k, nx)
        return Pair(
            lambda: remote(b2.at[to], r2.at[x], e2_s.at[n, k], e2_r.at[n, k], (to, s, y)),
            lambda: remote(b2.at[to], r2.at[frm], e2_s.at[n, k], e2_r.at[n, k], (to, s, y)),
        )

    def copy_y(part, k):
        to, frm = lax.rem(y + k, ny), lax.rem(y + ny - k, ny)
        at = pl.ds(0, tok) if part == 0 else pl.ds(tok, slots)
        return Pair(
            lambda: remote(cots.at[y, at], cots.at[y, at], yc_s.at[part, k], yc_r.at[part, k], (x, s, to)),
            lambda: remote(cots.at[y, at], cots.at[frm, at], yc_s.at[part, k], yc_r.at[part, k], (x, s, to)),
        )

    def copy_rs(grp, part, k):
        at = pl.ds(0, tok) if part == 0 else pl.ds(tok, slots)
        to = lax.rem(y + k, ny)
        return remote(
            rs_send.at[grp, k, at], rs_recv.at[grp, k, at], rs_s.at[grp, part, k], rs_r.at[grp, part, k], (x, s, to)
        )

    def copy_sum(n, k):
        to = lax.rem(y + k, ny)
        return remote(sum_send.at[n], sum_recv.at[n, k], sm_s.at[n, k], sm_r.at[n, k], (x, s, to))

    p = lax.broadcasted_iota(jnp.int32, (1, cols), 1)
    up_by = jnp.zeros_like(p)
    for j, (n, _) in enumerate(ORDER):
        up_by = jnp.where(lax.shift_right_arithmetic(p, jnp.full_like(p, 4)) == j, n + nz, up_by)
    place_of = ((z + up_by) & (nz - 1)) * 16 + (p & 15)
    reorder = jnp.where(lax.broadcasted_iota(jnp.int32, (cols, cols), 0) == place_of, 1.0, 0.0).astype(BF16)

    def to_pieces(v):
        return jnp.dot(v, reorder, preferred_element_type=F32).astype(BF16)

    def to_columns(v):
        return lax.dot_general(v, reorder, (((1,), (1,)), ((), ())), preferred_element_type=F32).astype(BF16)

    fetch[1].wait()
    fetch[2].wait()
    key_tok, pos_tok, own_tok = places(ts[...], shift_of(slots), nx, nseq)
    fill1(key_tok, cot[...], b1a, r1a)
    cots[y, :tok] = to_pieces(cot[...])

    def prepare(ref, base, lo, hi):
        def body(i):
            r = ref[pl.ds(pl.multiple_of(i * 16, 16), 16), :].astype(F32)
            at = pl.ds(pl.multiple_of(base + i * 16, 16), 16)
            xg[at, :] = (r * gain[...]).astype(BF16)
            sq[at, :] = jnp.broadcast_to(jnp.sum(r * r, axis=1, keepdims=True), (16, LANES))

        loop(lo, hi, body)

    work = {}
    for n in range(4):
        b = tok // 64
        work[2 + n] = [functools.partial(prepare, text, 0, n * b, (n + 1) * b)]
    for n in range(2):
        b = slots // 32
        work[6 + n] = [functools.partial(prepare, img, tok, n * b, (n + 1) * b)]

    def send_squares():
        sum_send[0] = jnp.transpose(sq[...])[:8]
        for k in range(1, ny):
            copy_sum(0, k).start()

    work[8] = [send_squares]

    def middle():
        loop(1, nseq, lambda k: copy1(0, b1a, r1a, k)[1].wait_recv())
        fill2(r1a, b2a, r2a)
        for k in range(1, nx):
            copy2(0, b2a, r2a, k)[0].start()

    work[9] = [middle]
    keys = []

    def slot_cots():
        keys.append(places(sd[...], shift_of(tok), nx, nseq))
        for k in range(1, nx):
            copy2(0, b2a, r2a, k)[1].wait_recv()
        cots[y, tok:] = to_pieces(take(keys[0][1], r2a).astype(BF16))
        for k in range(1, ny):
            copy_y(1, k)[0].start()

    work[13] = [slot_cots]

    def weights(t, grp, h):
        lo, hi = (0, nz) if grp is None else (grp * (nz // 2), (grp + 1) * (nz // 2))
        return wq[t, lo:hi, :, 8 * h : 8 * h + 8, :].reshape(16 * (hi - lo), half)

    dots = {0: jnp.zeros((tok, 1), F32), 1: jnp.zeros((slots, 1), F32)}

    def forward(grp):
        for j in range(grp * (nz // 2), (grp + 1) * (nz // 2)):
            copy_sib(j)[1].wait_recv()
        lanes = slice(grp * LANES, (grp + 1) * LANES)
        for part in (1, 0):
            lo, hi = (0, tok) if part == 0 else (tok, rows)
            v = jnp.zeros((hi - lo, ny * LANES), F32)
            for h in range(2):
                rhs = jnp.concatenate([weights(lax.rem(y + k, ny), grp, h) for k in range(ny)], axis=0)
                v = v + lax.dot_general(
                    xg[lo:hi, h * half : (h + 1) * half], rhs, (((1,), (1,)), ((), ())), preferred_element_type=F32
                )
            for k in (2, 1, 3, 0):
                u = v[:, k * LANES : (k + 1) * LANES]
                if k:
                    rs_send[grp, k, lo:hi] = u.astype(BF16)
                    copy_rs(grp, part, k).start()
                else:
                    kvp[lo:hi, lanes] = u
                near = cots[lax.rem(y + k, ny), lo:hi, lanes].astype(F32)
                dots[part] = dots[part] + jnp.sum(u * near, axis=1, keepdims=True)

    def forward_first():
        for part in range(2):
            for k in range(1, ny):
                copy_y(part, k)[1].wait_recv()
        forward(0)

    pieces = len(ORDER)
    work[pieces + LAG1 - 1] = [forward_first]
    for j in range(pieces + LAG2):
        if 1 <= j < 5:
            copy_z1(j)[1].wait_recv()
            copy_z2(1, j)[0].start()
            copy_z2(-1, j)[0].start()
            if j >= 3:
                copy_z8(j - 3)[0].start()
        elif 5 <= j < pieces - 1:
            copy_z2(*ORDER[j][1])[1].wait_recv()
        elif j == pieces - 1:
            copy_z8(0)[1].wait_recv()
            copy_z8(1)[1].wait_recv()
        if 1 <= j < pieces:
            copy_x(j, 0)[0].start()
            copy_x(j, 1)[0].start()
        if j == 4:
            loop(1, nseq, lambda k: copy1(0, b1a, r1a, k)[0].start())
            for k in range(1, ny):
                copy_y(0, k)[0].start()
        if LAG1 <= j < pieces + LAG1:
            i = j - LAG1
            copy_x(i, 0)[1].wait_recv()
            copy_x(i, 1)[1].wait_recv()
            copy_x(i, 2)[0].start()
        if LAG2 <= j:
            copy_x(j - LAG2, 2)[1].wait_recv()
            copy_sib(j - LAG2)[0].start()
        if j == 1:
            for f in fetch[3:]:
                f.wait()
        for f in work.get(j, ()):
            f()
    key_slot, pos_slot, own_slot = keys[0]

    total = sum_send[0]
    for k in range(1, ny):
        copy_sum(0, k).wait_recv()
        total = total + sum_recv[0, k]
    scale_r = lax.rsqrt(total[0:1] / D + EPS)
    sq[...] = jnp.transpose(jnp.broadcast_to(scale_r, (LANES, rows)))
    forward(1)

    def reduced(part):
        lo, hi = (0, tok) if part == 0 else (tok, rows)
        raw = kvp[lo:hi]
        for k in range(1, ny):
            for grp in range(2):
                copy_rs(grp, part, k).wait_recv()
            raw = raw + jnp.concatenate([rs_recv[0, k, lo:hi], rs_recv[1, k, lo:hi]], axis=1).astype(F32)
        return to_columns((raw * sq[lo:hi, 0:1]).astype(BF16))

    sum_send[1] = jnp.transpose(jnp.broadcast_to(jnp.concatenate([dots[0], dots[1]], axis=0), (rows, LANES)))[:8]
    for k in range(1, ny):
        copy_sum(1, k).start()

    fill1(key_slot, reduced(1), b1b, r1b)
    loop(1, nseq, lambda k: copy1(1, b1b, r1b, k)[0].start())

    cot_all = jnp.concatenate([cots[t] for t in range(ny)], axis=1)
    for h in range(2):
        rhs = jnp.concatenate([weights(t, None, h) for t in range(ny)], axis=0)
        acc[:, h * half : (h + 1) * half] = jnp.dot(cot_all, rhs, preferred_element_type=F32)

    total = sum_send[1]
    for k in range(1, ny):
        copy_sum(1, k).wait_recv()
        total = total + sum_recv[1, k]
    coef_r = scale_r * scale_r * scale_r * total[0:1] / D
    coef = jnp.transpose(jnp.broadcast_to(coef_r, (LANES, rows)))
    keep = jnp.concatenate([jnp.where(own_tok < 0.0, 1.0, 0.0), jnp.where(own_slot >= 0.0, 1.0, 0.0)], axis=0)
    lane = lax.broadcasted_iota(jnp.int32, (rows, LANES), 1)
    sq[...] = jnp.where(lane == 0, sq[...], jnp.where(lane == 1, coef, keep))

    def grads(ref, base, out):
        def body(i):
            here = pl.ds(pl.multiple_of(i * 16, 16), 16)
            at = pl.ds(pl.multiple_of(base + i * 16, 16), 16)
            r = ref[here, :].astype(F32)
            f = sq[at, :]
            g = f[:, 0:1] * (gain[...] * acc[at, :]) - r * f[:, 1:2]
            out[here, :] = jnp.where(f[:, 2:3] > 0.0, g, 0.0).astype(BF16)

        loop(0, ref.shape[0] // 16, body)

    loop(1, nseq, lambda k: copy1(1, b1b, r1b, k)[1].wait_recv())
    fill2(r1b, b2b, r2b)
    for k in range(1, nx):
        copy2(1, b2b, r2b, k)[0].start()
    grads(text, 0, tg_out)
    grads(img, tok, ig_out)
    kv_text = reduced(0)
    for i in range(1, 5):
        copy_z1(i)[0].wait_send()
    for i in range(5):
        copy_z2(1, i)[0].wait_send()
        copy_z2(-1, i)[0].wait_send()
    for m in range(2):
        copy_z8(m)[0].wait_send()
    for j in range(pieces):
        for m in range(3):
            copy_x(j, m)[0].wait_send()
        copy_sib(j)[0].wait_send()
    for k in range(1, nx):
        copy2(0, b2a, r2a, k)[0].wait_send()
    for k in range(1, ny):
        for part in range(2):
            copy_y(part, k)[0].wait_send()
            copy_rs(0, part, k).wait_send()
            copy_rs(1, part, k).wait_send()
            copy_sum(part, k).wait_send()

    def sent1(k):
        copy1(0, b1a, r1a, k)[0].wait_send()
        copy1(1, b1b, r1b, k)[0].wait_send()

    loop(1, nseq, sent1)

    for k in range(1, nx):
        copy2(1, b2b, r2b, k)[1].wait_recv()
    got = take(pos_tok, r2b)
    kv_out[...] = jnp.where(own_tok >= 0.0, got, kv_text.astype(F32)).astype(BF16)
    for k in range(1, nx):
        copy2(1, b2b, r2b, k)[0].wait_send()


def flush(a, b, c, out_a, out_b, out_c, via_a, via_b, via_c, sem):
    ways = ((b, via_b, out_b), (c, via_c, out_c), (a, via_a, out_a))
    into = [pltpu.make_async_copy(p, v, sem.at[0, i]) for i, (p, v, _) in enumerate(ways)]
    away = [pltpu.make_async_copy(v, q, sem.at[1, i]) for i, (_, v, q) in enumerate(ways)]
    for p in into:
        p.start()
    for p, q in zip(into, away):
        p.wait()
        q.start()
    for q in away:
        q.wait()


def per_device(text_embed, image_rows, token_source, slot_dest, norm_gain, kv_weight, kv_cot):
    nx, nseq, ny = lax.axis_size("sec"), lax.axis_size("seq"), lax.axis_size("tp")
    nz = nseq // 2
    tok, feat = text_embed.shape
    slots = image_rows.shape[0]
    rows = tok + slots
    cols = kv_cot.shape[1]
    dma = pltpu.SemaphoreType.DMA
    blk = (2 * nx * cols) // LANES
    exch = [
        pltpu.VMEM((nseq, blk, LANES), BF16),
        pltpu.VMEM((nseq, blk, LANES), BF16),
        pltpu.VMEM((nx, 2 * nseq, cols), BF16),
        pltpu.VMEM((nx, 2 * nseq, cols), BF16),
    ]
    vmem = pl.BlockSpec(memory_space=pltpu.VMEM)
    outs = pl.pallas_call(
        functools.partial(kernel, nx, nz, ny),
        out_shape=(
            jax.ShapeDtypeStruct((tok, cols), BF16),
            jax.ShapeDtypeStruct((tok, feat), BF16),
            jax.ShapeDtypeStruct((slots, feat), BF16),
        ),
        in_specs=[pl.BlockSpec(memory_space=pl.ANY)] * 7,
        out_specs=(vmem, vmem, vmem),
        scratch_shapes=[
            pltpu.VMEM((tok, feat), BF16),
            pltpu.VMEM((slots, feat), BF16),
            pltpu.VMEM((1, tok), jnp.int32),
            pltpu.VMEM((1, slots), jnp.int32),
            pltpu.VMEM((1, feat), F32),
            pltpu.VMEM((8, feat), BF16),
            pltpu.VMEM((tok, cols), BF16),
            pltpu.VMEM((nx, nz, 2, 16, feat // 2), BF16),
            pltpu.VMEM((rows, feat), BF16),
            pltpu.VMEM((ny, rows, cols), BF16),
            pltpu.VMEM((rows, LANES), F32),
            pltpu.VMEM((rows, feat), F32),
            pltpu.VMEM((rows, cols), F32),
            pltpu.VMEM((2, ny, rows, LANES), BF16),
            pltpu.VMEM((2, ny, rows, LANES), BF16),
            pltpu.VMEM((2, 8, rows), F32),
            pltpu.VMEM((2, ny, 8, rows), F32),
            *exch,
            *exch,
            dma((7,)),
            *[dma((5,))] * 2,
            *[dma((2, 5))] * 2,
            *[dma((2,))] * 2,
            *[dma((nz, 3))] * 2,
            *[dma((nz,))] * 2,
            *[dma((2, nseq))] * 2,
            *[dma((2, nx))] * 2,
            *[dma((2, ny))] * 2,
            *[dma((2, 2, ny))] * 2,
            *[dma((2, ny))] * 2,
        ],
        compiler_params=pltpu.CompilerParams(
            collective_id=0, has_side_effects=True, vmem_limit_bytes=58 * 2**20
        ),
        cost_estimate=pl.CostEstimate(
            flops=4 * rows * feat * cols * ny, bytes_accessed=8 * rows * feat, transcendentals=0
        ),
    )(
        text_embed,
        image_rows,
        token_source.reshape(1, tok),
        slot_dest.reshape(1, slots),
        norm_gain.reshape(1, feat),
        kv_weight,
        kv_cot,
    )
    where = pl.BlockSpec(memory_space=pl.ANY)
    return pl.pallas_call(
        flush,
        out_shape=tuple(jax.ShapeDtypeStruct(o.shape, o.dtype) for o in outs),
        in_specs=[where] * 3,
        out_specs=(where,) * 3,
        scratch_shapes=[*[pltpu.VMEM(o.shape, o.dtype) for o in outs], dma((2, 3))],
        compiler_params=pltpu.CompilerParams(vmem_limit_bytes=58 * 2**20),
    )(*outs)


def solution(mesh):
    both = P(("sec", "seq"), "tp")
    rows = P(("sec", "seq"))
    return jax.shard_map(
        per_device,
        mesh=mesh,
        in_specs=(both, both, rows, rows, P("tp"), both, both),
        out_specs=(both, both, both),
        check_vma=False,
    )
```

time: 238 us -> 84.5 us (0.36)
  waiting for transfers between devices: 144 us -> 0 us
  Pallas kernels: 0 us -> 83.7 us
  starting transfers between devices: 38 us -> 0 us
  blocking collectives: 19.9 us -> 0 us
  between operations: 14.1 us -> 0.64 us
  matrix products: 12.3 us -> 0 us
  other arithmetic: 7.43 us -> 0 us
    all_gather x1 -> x0, waiting for transfers between devices: 97.1 us -> none  [per_device(): weight = lax.all_gather(kv_weight, axes, axis=0, tiled=True)]
    pallas_call x0 -> x2, Pallas kernels: none -> 83.7 us  [the longest x1 81.3 us: per_device(): pl.pallas_call(functools.partial(kernel, nx, nz, ny), out_shape=(jax.Shap...]
    all_to_all x2 -> x0, starting transfers between devices: 37.9 us -> none  [move(): got = lax.all_to_all(send, axes, split_axis=0, concat_axis=0, tiled=True)]
    all_to_all x2 -> x0, waiting for transfers between devices: 31.4 us -> none  [move(): got = lax.all_to_all(send, axes, split_axis=0, concat_axis=0, tiled=True)]
    reduce_scatter x1 -> x0, waiting for transfers between devices: 14.7 us -> none  [per_device(): raw = lax.psum_scatter(partial, 'tp', scatter_dimension=1, tiled=True)]
    dot_general x6 -> x0, matrix products: 12.3 us -> none  [the longest x1 5.7 us: per_device(): lax.dot_general(gained, weight, (((1,), (1,)), ((), ())), preferred_eleme...]
    all_gather x1 -> x0, blocking collectives: 11.4 us -> none  [per_device(): lax.all_gather(jnp.concatenate([kv_cot, cot_img]), 'tp', axis=1, tiled=True)]
    psum x1 -> x0, blocking collectives: 8.46 us -> none  [per_device(): sumsq, dots = lax.psum(sums, 'tp')]
  transfers between devices with their start and end apart: 4 -> 0, of which waited for: 4 -> 0; matrix products, arithmetic and copies ran while one was open for 5% -> 0% of each run, Pallas kernels for 0% -> 0%
where the time goes in v3:
time: 84.5 us; the launch traced here: 84.4 us
  Pallas kernels  83.7 us (99%)
    pallas_call x1, Pallas kernels, per_device(): pl.pallas_call(functools.partial(kernel, nx, nz, ny), out_shape=(jax.Shap...  81.3 us
    pallas_call x1, Pallas kernels, per_device(): pl.pallas_call(flush, out_shape=tuple((jax.ShapeDtypeStruct(o.shape, o.dt...  2.45 us

profile of v3, /device:TPU:1, one launch (start us, length us, event | category | flops | bytes accessed | tf_op | source)
XLA Modules:
  0.0 84.4 jit_solution(17658811588644472601)
XLA Ops:
  0.6 81.3 %shard_map.94 = (bf16[256,256]{1,0:T(8,128)(2,1)}, bf16[256,2048]{1,0:T(8,128)(2,1)}, bf16[128,2048]{1,0:T(8,128)(2,1)}) custom-call(bf16[256,2048]{1,0:T(8,128)(2,1)} %text_h.1, bf16[128,2048]{1,0:T(8,128)(2,1)} %img_h.1, s32[1,256]{1,0:T(1,128)} %bitcast.4, s32[1,128]{1,0:T(1,128)} %bitcast.5, f32[1,2048]{1,0:T(1,128)} %bitcast.3, bf16[8,2048]{1,0:T(8,128)(2,1)} %w_h.1, ...), custom_call_target="tpu_custom_call" | custom-call | flops 3221225472 | bytes 6291456 | tf_op jit(solution)/shard_map/pallas_call | solution.py:481
  81.9 2.5 %shard_map.95 = (bf16[256,256]{1,0:T(8,128)(2,1)}, bf16[256,2048]{1,0:T(8,128)(2,1)}, bf16[128,2048]{1,0:T(8,128)(2,1)}) custom-call(bf16[256,256]{1,0:T(8,128)(2,1)} %get-tuple-element.6.a, bf16[256,2048]{1,0:T(8,128)(2,1)} %get-tuple-element.7.b, bf16[128,2048]{1,0:T(8,128)(2,1)} %get-tuple-element.8.c), custom_call_target="tpu_custom_call" | custom-call | tf_op jit(solution)/shard_map/pallas_call | solution.py:538

commit v4 on v3

--- a/solution.py
+++ b/solution.py
@@ -46,8 +46,13 @@
 
 
 NEAR = (0, 3, -3, 6, -6)
-ORDER = [(0, None)] + [(n, None) for n in NEAR[1:]] + [(n + e, (e, i)) for i, n in enumerate(NEAR) for e in (1, -1)] + [(8, None)]
-LAG1, LAG2 = 3, 6
+ORDER = (
+    [(0, (0, 0)), (1, (1, 0)), (-1, (-1, 0))]
+    + [(NEAR[i], (0, i)) for i in range(1, 5)]
+    + [(NEAR[i] + e, (e, i)) for i in range(1, 5) for e in (1, -1)]
+    + [(8, None)]
+)
+LAG1, LAG2, EXCH = 3, 6, 12
 SLOT = {(n + 16) % 16: j for j, (n, _) in enumerate(ORDER)}
 
 
@@ -56,7 +61,7 @@
     text_h, img_h, ts_h, sd_h, gain_h, w_h, cot_h,
     kv_out, tg_out, ig_out,
     text, img, ts, sd, gain, w, cot,
-    wq, xg, cots, sq, acc, kvp, rs_send, rs_recv, sum_send, sum_recv,
+    wq, xg, cots, sq, acc, vs, kvp, rs_send, rs_recv, sum_send, sum_recv,
     b1a, r1a, b2a, r2a, b1b, r1b, b2b, r2b,
     in_sem, z1_s, z1_r, z2_s, z2_r, z8_s, z8_r, x_s, x_r, sib_s, sib_r,
     e1_s, e1_r, e2_s, e2_r, yc_s, yc_r, rs_s, rs_r, sm_s, sm_r,
@@ -107,7 +112,7 @@
 
     def copy_z1(i):
         n = NEAR[i]
-        own, got = wq.at[x, 0, c], wq.at[x, i, c]
+        own, got = wq.at[x, 0, c], wq.at[x, SLOT[n % 16], c]
         dev = (x, 2 * at_z(-n) + c, y)
         return Pair(
             lambda: remote(own, got, z1_s.at[i], z1_r.at[i], dev),
@@ -116,7 +121,7 @@
 
     def copy_z2(e, i):
         n, m = NEAR[i], (1 - e) // 2
-        out, got = wq.at[x, i, c], wq.at[x, SLOT[(n + e) % 16], c]
+        out, got = wq.at[x, SLOT[n % 16], c], wq.at[x, SLOT[(n + e) % 16], c]
         dev = (x, 2 * at_z(-e) + c, y)
         return Pair(
             lambda: remote(out, got, z2_s.at[m, i], z2_r.at[m, i], dev),
@@ -124,9 +129,9 @@
         )
 
     def copy_z8(m):
-        n, to = (3, -2) if m == 0 else (4, 2)
+        n, to = (6, -2) if m == 0 else (-6, 2)
         part = pl.ds(m * (half // 2), half // 2)
-        out, got = wq.at[x, n, c, :, part], wq.at[x, SLOT[8], c, :, part]
+        out, got = wq.at[x, SLOT[n % 16], c, :, part], wq.at[x, SLOT[8], c, :, part]
         dev = (x, 2 * at_z(to) + c, y)
         return Pair(
             lambda: remote(out, got, z8_s.at[m], z8_r.at[m], dev),
@@ -155,12 +160,12 @@
     w8 = w[...].astype(F32)
     wq[x, 0, c] = jnp.concatenate([w8[:, :half], w8[:, half:]], axis=0).astype(BF16)
     pl.semaphore_wait(barrier, nseq - 1 + nx - 1 + ny - 1)
+    copy_z2(1, 0)[0].start()
+    copy_z2(-1, 0)[0].start()
+    copy_x(0, 0)[0].start()
+    copy_x(0, 1)[0].start()
     for i in range(1, 5):
         copy_z1(i)[0].start()
-    copy_x(0, 0)[0].start()
-    copy_x(0, 1)[0].start()
-    copy_z2(1, 0)[0].start()
-    copy_z2(-1, 0)[0].start()
 
     def pick_rows(key):
         n = key.shape[1]
@@ -275,7 +280,7 @@
         for k in range(1, nx):
             copy2(0, b2a, r2a, k)[0].start()
 
-    work[9] = [middle]
+    work[19] = [middle]
     keys = []
 
     def slot_cots():
@@ -286,13 +291,10 @@
         for k in range(1, ny):
             copy_y(1, k)[0].start()
 
-    work[13] = [slot_cots]
 
     def weights(t, grp, h):
         lo, hi = (0, nz) if grp is None else (grp * (nz // 2), (grp + 1) * (nz // 2))
         return wq[t, lo:hi, :, 8 * h : 8 * h + 8, :].reshape(16 * (hi - lo), half)
-
-    dots = {0: jnp.zeros((tok, 1), F32), 1: jnp.zeros((slots, 1), F32)}
 
     def forward(grp):
         for j in range(grp * (nz // 2), (grp + 1) * (nz // 2)):
@@ -313,36 +315,32 @@
                     copy_rs(grp, part, k).start()
                 else:
                     kvp[lo:hi, lanes] = u
-                near = cots[lax.rem(y + k, ny), lo:hi, lanes].astype(F32)
-                dots[part] = dots[part] + jnp.sum(u * near, axis=1, keepdims=True)
-
-    def forward_first():
-        for part in range(2):
-            for k in range(1, ny):
-                copy_y(part, k)[1].wait_recv()
-        forward(0)
+                vs[grp, k, lo:hi] = u
 
     pieces = len(ORDER)
-    work[pieces + LAG1 - 1] = [forward_first]
+    work.setdefault(pieces + LAG1 - 1, []).append(functools.partial(forward, 0))
     for j in range(pieces + LAG2):
-        if 1 <= j < 5:
-            copy_z1(j)[1].wait_recv()
-            copy_z2(1, j)[0].start()
-            copy_z2(-1, j)[0].start()
-            if j >= 3:
-                copy_z8(j - 3)[0].start()
-        elif 5 <= j < pieces - 1:
-            copy_z2(*ORDER[j][1])[1].wait_recv()
-        elif j == pieces - 1:
-            copy_z8(0)[1].wait_recv()
-            copy_z8(1)[1].wait_recv()
         if 1 <= j < pieces:
+            come = ORDER[j][1]
+            if come is None:
+                copy_z8(0)[1].wait_recv()
+                copy_z8(1)[1].wait_recv()
+            elif come[0]:
+                copy_z2(*come)[1].wait_recv()
+            else:
+                i = come[1]
+                copy_z1(i)[1].wait_recv()
+                copy_z2(1, i)[0].start()
+                copy_z2(-1, i)[0].start()
+                if i >= 3:
+                    copy_z8(i - 3)[0].start()
             copy_x(j, 0)[0].start()
             copy_x(j, 1)[0].start()
-        if j == 4:
-            loop(1, nseq, lambda k: copy1(0, b1a, r1a, k)[0].start())
+        if j == 8:
             for k in range(1, ny):
                 copy_y(0, k)[0].start()
+        if j == EXCH:
+            loop(1, nseq, lambda k: copy1(0, b1a, r1a, k)[0].start())
         if LAG1 <= j < pieces + LAG1:
             i = j - LAG1
             copy_x(i, 0)[1].wait_recv()
@@ -356,7 +354,6 @@
                 f.wait()
         for f in work.get(j, ()):
             f()
-    key_slot, pos_slot, own_slot = keys[0]
 
     total = sum_send[0]
     for k in range(1, ny):
@@ -365,6 +362,8 @@
     scale_r = lax.rsqrt(total[0:1] / D + EPS)
     sq[...] = jnp.transpose(jnp.broadcast_to(scale_r, (LANES, rows)))
     forward(1)
+    slot_cots()
+    key_slot, pos_slot, own_slot = keys[0]
 
     def reduced(part):
         lo, hi = (0, tok) if part == 0 else (tok, rows)
@@ -375,12 +374,21 @@
             raw = raw + jnp.concatenate([rs_recv[0, k, lo:hi], rs_recv[1, k, lo:hi]], axis=1).astype(F32)
         return to_columns((raw * sq[lo:hi, 0:1]).astype(BF16))
 
-    sum_send[1] = jnp.transpose(jnp.broadcast_to(jnp.concatenate([dots[0], dots[1]], axis=0), (rows, LANES)))[:8]
+    fill1(key_slot, reduced(1), b1b, r1b)
+    for k in range(1, nseq):
+        copy1(1, b1b, r1b, k)[0].start()
+
+    for part in range(2):
+        for k in range(1, ny):
+            copy_y(part, k)[1].wait_recv()
+    dots = jnp.zeros((rows, LANES), F32)
+    for k in range(ny):
+        near = cots[lax.rem(y + k, ny)].astype(F32)
+        for grp in range(2):
+            dots = dots + vs[grp, k] * near[:, grp * LANES : (grp + 1) * LANES]
+    sum_send[1] = jnp.transpose(jnp.broadcast_to(jnp.sum(dots, axis=1, keepdims=True), (rows, LANES)))[:8]
     for k in range(1, ny):
         copy_sum(1, k).start()
-
-    fill1(key_slot, reduced(1), b1b, r1b)
-    loop(1, nseq, lambda k: copy1(1, b1b, r1b, k)[0].start())
 
     cot_all = jnp.concatenate([cots[t] for t in range(ny)], axis=1)
     for h in range(2):
@@ -500,6 +508,7 @@
             pltpu.VMEM((ny, rows, cols), BF16),
             pltpu.VMEM((rows, LANES), F32),
             pltpu.VMEM((rows, feat), F32),
+            pltpu.VMEM((2, ny, rows, LANES), F32),
             pltpu.VMEM((rows, cols), F32),
             pltpu.VMEM((2, ny, rows, LANES), BF16),
             pltpu.VMEM((2, ny, rows, LANES), BF16),

time: 84.5 us -> 74.7 us (0.88)
  Pallas kernels: 83.7 us -> 73.9 us
    pallas_call x1, Pallas kernels: 81.3 us -> 71.4 us  [per_device(): pl.pallas_call(functools.partial(kernel, nx, nz, ny), out_shape=(jax.Shap...]
where the time goes in v4:
time: 74.7 us; the launch traced here: 74.5 us
  Pallas kernels  73.9 us (99%)
    pallas_call x1, Pallas kernels, per_device(): pl.pallas_call(functools.partial(kernel, nx, nz, ny), out_shape=(jax.Shap...  71.4 us
    pallas_call x1, Pallas kernels, per_device(): pl.pallas_call(flush, out_shape=tuple((jax.ShapeDtypeStruct(o.shape, o.dt...  2.45 us

profile of v4, /device:TPU:1, one launch (start us, length us, event | category | flops | bytes accessed | tf_op | source)
XLA Modules:
  0.0 74.5 jit_solution(5872880613925952920)
XLA Ops:
  0.6 71.4 %shard_map.94 = (bf16[256,256]{1,0:T(8,128)(2,1)}, bf16[256,2048]{1,0:T(8,128)(2,1)}, bf16[128,2048]{1,0:T(8,128)(2,1)}) custom-call(bf16[256,2048]{1,0:T(8,128)(2,1)} %text_h.1, bf16[128,2048]{1,0:T(8,128)(2,1)} %img_h.1, s32[1,256]{1,0:T(1,128)} %bitcast.4, s32[1,128]{1,0:T(1,128)} %bitcast.5, f32[1,2048]{1,0:T(1,128)} %bitcast.3, bf16[8,2048]{1,0:T(8,128)(2,1)} %w_h.1, ...), custom_call_target="tpu_custom_call" | custom-call | flops 3221225472 | bytes 6291456 | tf_op jit(solution)/shard_map/pallas_call | solution.py:489
  72.1 2.5 %shard_map.95 = (bf16[256,256]{1,0:T(8,128)(2,1)}, bf16[256,2048]{1,0:T(8,128)(2,1)}, bf16[128,2048]{1,0:T(8,128)(2,1)}) custom-call(bf16[256,256]{1,0:T(8,128)(2,1)} %get-tuple-element.6.a, bf16[256,2048]{1,0:T(8,128)(2,1)} %get-tuple-element.7.b, bf16[128,2048]{1,0:T(8,128)(2,1)} %get-tuple-element.8.c), custom_call_target="tpu_custom_call" | custom-call | tf_op jit(solution)/shard_map/pallas_call | solution.py:547

commit v5 on v4

--- a/solution.py
+++ b/solution.py
@@ -45,11 +45,13 @@
     return key, pos, own_col
 
 
-NEAR = (0, 3, -3, 6, -6)
+NEAR = (0, 5, -5)
+STEPS = (1, -1, 2, -2)
 ORDER = (
-    [(0, (0, 0)), (1, (1, 0)), (-1, (-1, 0))]
-    + [(NEAR[i], (0, i)) for i in range(1, 5)]
-    + [(NEAR[i] + e, (e, i)) for i in range(1, 5) for e in (1, -1)]
+    [(0, (0, 0))]
+    + [(e, (e, 0)) for e in STEPS]
+    + [(NEAR[i], (0, i)) for i in (1, 2)]
+    + [(NEAR[i] + e, (e, i)) for e in STEPS for i in (1, 2)]
     + [(8, None)]
 )
 LAG1, LAG2, EXCH = 3, 6, 12
@@ -59,11 +61,12 @@
 def kernel(
     nx, nz, ny,
     text_h, img_h, ts_h, sd_h, gain_h, w_h, cot_h,
+    kv_h, tg_h, ig_h,
     kv_out, tg_out, ig_out,
     text, img, ts, sd, gain, w, cot,
     wq, xg, cots, sq, acc, vs, kvp, rs_send, rs_recv, sum_send, sum_recv,
     b1a, r1a, b2a, r2a, b1b, r1b, b2b, r2b,
-    in_sem, z1_s, z1_r, z2_s, z2_r, z8_s, z8_r, x_s, x_r, sib_s, sib_r,
+    out_sem, in_sem, z1_s, z1_r, z2_s, z2_r, z8_s, z8_r, x_s, x_r, sib_s, sib_r,
     e1_s, e1_r, e2_s, e2_r, yc_s, yc_r, rs_s, rs_r, sm_s, sm_r,
 ):
     x, s, y = lax.axis_index("sec"), lax.axis_index("seq"), lax.axis_index("tp")
@@ -120,7 +123,7 @@
         )
 
     def copy_z2(e, i):
-        n, m = NEAR[i], (1 - e) // 2
+        n, m = NEAR[i], STEPS.index(e)
         out, got = wq.at[x, SLOT[n % 16], c], wq.at[x, SLOT[(n + e) % 16], c]
         dev = (x, 2 * at_z(-e) + c, y)
         return Pair(
@@ -129,7 +132,7 @@
         )
 
     def copy_z8(m):
-        n, to = (6, -2) if m == 0 else (-6, 2)
+        n, to = (5, -3) if m == 0 else (-5, 3)
         part = pl.ds(m * (half // 2), half // 2)
         out, got = wq.at[x, SLOT[n % 16], c, :, part], wq.at[x, SLOT[8], c, :, part]
         dev = (x, 2 * at_z(to) + c, y)
@@ -164,8 +167,10 @@
     copy_z2(-1, 0)[0].start()
     copy_x(0, 0)[0].start()
     copy_x(0, 1)[0].start()
-    for i in range(1, 5):
+    for i in range(1, 3):
         copy_z1(i)[0].start()
+    copy_z2(2, 0)[0].start()
+    copy_z2(-2, 0)[0].start()
 
     def pick_rows(key):
         n = key.shape[1]
@@ -262,17 +267,17 @@
     work = {}
     for n in range(4):
         b = tok // 64
-        work[2 + n] = [functools.partial(prepare, text, 0, n * b, (n + 1) * b)]
+        work[9 + n] = [functools.partial(prepare, text, 0, n * b, (n + 1) * b)]
     for n in range(2):
         b = slots // 32
-        work[6 + n] = [functools.partial(prepare, img, tok, n * b, (n + 1) * b)]
+        work[13 + n] = [functools.partial(prepare, img, tok, n * b, (n + 1) * b)]
 
     def send_squares():
         sum_send[0] = jnp.transpose(sq[...])[:8]
         for k in range(1, ny):
             copy_sum(0, k).start()
 
-    work[8] = [send_squares]
+    work[15] = [send_squares]
 
     def middle():
         loop(1, nseq, lambda k: copy1(0, b1a, r1a, k)[1].wait_recv())
@@ -281,10 +286,10 @@
             copy2(0, b2a, r2a, k)[0].start()
 
     work[19] = [middle]
+    work[21] = [lambda: loop(1, nseq, lambda k: copy1(0, b1a, r1a, k)[0].wait_send())]
     keys = []
 
     def slot_cots():
-        keys.append(places(sd[...], shift_of(tok), nx, nseq))
         for k in range(1, nx):
             copy2(0, b2a, r2a, k)[1].wait_recv()
         cots[y, tok:] = to_pieces(take(keys[0][1], r2a).astype(BF16))
@@ -312,10 +317,20 @@
                 u = v[:, k * LANES : (k + 1) * LANES]
                 if k:
                     rs_send[grp, k, lo:hi] = u.astype(BF16)
-                    copy_rs(grp, part, k).start()
+                    if (grp, part) != (1, 0):
+                        copy_rs(grp, part, k).start()
                 else:
                     kvp[lo:hi, lanes] = u
                 vs[grp, k, lo:hi] = u
+
+    def sent_z():
+        for i in range(1, 3):
+            copy_z1(i)[0].wait_send()
+        for i in range(3):
+            for e in STEPS:
+                copy_z2(e, i)[0].wait_send()
+        for m in range(2):
+            copy_z8(m)[0].wait_send()
 
     pieces = len(ORDER)
     work.setdefault(pieces + LAG1 - 1, []).append(functools.partial(forward, 0))
@@ -330,10 +345,9 @@
             else:
                 i = come[1]
                 copy_z1(i)[1].wait_recv()
-                copy_z2(1, i)[0].start()
-                copy_z2(-1, i)[0].start()
-                if i >= 3:
-                    copy_z8(i - 3)[0].start()
+                for e in STEPS:
+                    copy_z2(e, i)[0].start()
+                copy_z8(i - 1)[0].start()
             copy_x(j, 0)[0].start()
             copy_x(j, 1)[0].start()
         if j == 8:
@@ -349,6 +363,10 @@
         if LAG2 <= j:
             copy_x(j - LAG2, 2)[1].wait_recv()
             copy_sib(j - LAG2)[0].start()
+            for m in range(2):
+                copy_x(j - LAG2, m)[0].wait_send()
+        if j == pieces:
+            sent_z()
         if j == 1:
             for f in fetch[3:]:
                 f.wait()
@@ -362,7 +380,7 @@
     scale_r = lax.rsqrt(total[0:1] / D + EPS)
     sq[...] = jnp.transpose(jnp.broadcast_to(scale_r, (LANES, rows)))
     forward(1)
-    slot_cots()
+    keys.append(places(sd[...], shift_of(tok), nx, nseq))
     key_slot, pos_slot, own_slot = keys[0]
 
     def reduced(part):
@@ -377,10 +395,21 @@
     fill1(key_slot, reduced(1), b1b, r1b)
     for k in range(1, nseq):
         copy1(1, b1b, r1b, k)[0].start()
-
-    for part in range(2):
-        for k in range(1, ny):
-            copy_y(part, k)[1].wait_recv()
+    slot_cots()
+    for k in (2, 1, 3):
+        copy_rs(1, 0, k).start()
+
+    def backward(lo, hi):
+        cot_all = jnp.concatenate([cots[t, lo:hi] for t in range(ny)], axis=1)
+        for h in range(2):
+            rhs = jnp.concatenate([weights(t, None, h) for t in range(ny)], axis=0)
+            acc[lo:hi, h * half : (h + 1) * half] = jnp.dot(cot_all, rhs, preferred_element_type=F32)
+
+    for k in range(1, ny):
+        copy_y(0, k)[1].wait_recv()
+    backward(0, tok)
+    for k in range(1, ny):
+        copy_y(1, k)[1].wait_recv()
     dots = jnp.zeros((rows, LANES), F32)
     for k in range(ny):
         near = cots[lax.rem(y + k, ny)].astype(F32)
@@ -389,11 +418,7 @@
     sum_send[1] = jnp.transpose(jnp.broadcast_to(jnp.sum(dots, axis=1, keepdims=True), (rows, LANES)))[:8]
     for k in range(1, ny):
         copy_sum(1, k).start()
-
-    cot_all = jnp.concatenate([cots[t] for t in range(ny)], axis=1)
-    for h in range(2):
-        rhs = jnp.concatenate([weights(t, None, h) for t in range(ny)], axis=0)
-        acc[:, h * half : (h + 1) * half] = jnp.dot(cot_all, rhs, preferred_element_type=F32)
+    backward(tok, rows)
 
     total = sum_send[1]
     for k in range(1, ny):
@@ -404,6 +429,9 @@
     keep = jnp.concatenate([jnp.where(own_tok < 0.0, 1.0, 0.0), jnp.where(own_slot >= 0.0, 1.0, 0.0)], axis=0)
     lane = lax.broadcasted_iota(jnp.int32, (rows, LANES), 1)
     sq[...] = jnp.where(lane == 0, sq[...], jnp.where(lane == 1, coef, keep))
+
+    results = ((tg_out, tg_h), (ig_out, ig_h), (kv_out, kv_h))
+    done = [pltpu.make_async_copy(p, q, out_sem.at[i]) for i, (p, q) in enumerate(results)]
 
     def grads(ref, base, out):
         def body(i):
@@ -421,18 +449,12 @@
     for k in range(1, nx):
         copy2(1, b2b, r2b, k)[0].start()
     grads(text, 0, tg_out)
+    done[0].start()
     grads(img, tok, ig_out)
+    done[1].start()
     kv_text = reduced(0)
-    for i in range(1, 5):
-        copy_z1(i)[0].wait_send()
-    for i in range(5):
-        copy_z2(1, i)[0].wait_send()
-        copy_z2(-1, i)[0].wait_send()
-    for m in range(2):
-        copy_z8(m)[0].wait_send()
     for j in range(pieces):
-        for m in range(3):
-            copy_x(j, m)[0].wait_send()
+        copy_x(j, 2)[0].wait_send()
         copy_sib(j)[0].wait_send()
     for k in range(1, nx):
         copy2(0, b2a, r2a, k)[0].wait_send()
@@ -444,7 +466,6 @@
             copy_sum(part, k).wait_send()
 
     def sent1(k):
-        copy1(0, b1a, r1a, k)[0].wait_send()
         copy1(1, b1b, r1b, k)[0].wait_send()
 
     loop(1, nseq, sent1)
@@ -453,6 +474,9 @@
         copy2(1, b2b, r2b, k)[1].wait_recv()
     got = take(pos_tok, r2b)
     kv_out[...] = jnp.where(own_tok >= 0.0, got, kv_text.astype(F32)).astype(BF16)
+    done[2].start()
+    for d in done:
+        d.wait()
     for k in range(1, nx):
         copy2(1, b2b, r2b, k)[0].wait_send()
 
@@ -485,7 +509,7 @@
         pltpu.VMEM((nx, 2 * nseq, cols), BF16),
         pltpu.VMEM((nx, 2 * nseq, cols), BF16),
     ]
-    vmem = pl.BlockSpec(memory_space=pltpu.VMEM)
+    hbm = pl.BlockSpec(memory_space=pl.ANY)
     outs = pl.pallas_call(
         functools.partial(kernel, nx, nz, ny),
         out_shape=(
@@ -494,8 +518,11 @@
             jax.ShapeDtypeStruct((slots, feat), BF16),
         ),
         in_specs=[pl.BlockSpec(memory_space=pl.ANY)] * 7,
-        out_specs=(vmem, vmem, vmem),
+        out_specs=(hbm, hbm, hbm),
         scratch_shapes=[
+            pltpu.VMEM((tok, cols), BF16),
+            pltpu.VMEM((tok, feat), BF16),
+            pltpu.VMEM((slots, feat), BF16),
             pltpu.VMEM((tok, feat), BF16),
             pltpu.VMEM((slots, feat), BF16),
             pltpu.VMEM((1, tok), jnp.int32),
@@ -516,9 +543,10 @@
             pltpu.VMEM((2, ny, 8, rows), F32),
             *exch,
             *exch,
+            dma((3,)),
             dma((7,)),
-            *[dma((5,))] * 2,
-            *[dma((2, 5))] * 2,
+            *[dma((3,))] * 2,
+            *[dma((4, 3))] * 2,
             *[dma((2,))] * 2,
             *[dma((nz, 3))] * 2,
             *[dma((nz,))] * 2,

time: 74.7 us -> 72.9 us (0.976)
  Pallas kernels: 73.9 us -> 72.1 us
    pallas_call x1, Pallas kernels: 71.4 us -> 69.6 us  [per_device(): pl.pallas_call(functools.partial(kernel, nx, nz, ny), out_shape=(jax.Shap...]
where the time goes in v5:
time: 72.9 us; the launch traced here: 72.7 us
  Pallas kernels  72.1 us (99%)
    pallas_call x1, Pallas kernels, per_device(): pl.pallas_call(functools.partial(kernel, nx, nz, ny), out_shape=(jax.Shap...  69.6 us
    pallas_call x1, Pallas kernels, per_device(): pl.pallas_call(flush, out_shape=tuple((jax.ShapeDtypeStruct(o.shape, o.dt...  2.45 us

profile of v5, /device:TPU:1, one launch (start us, length us, event | category | flops | bytes accessed | tf_op | source)
XLA Modules:
  0.0 72.7 jit_solution(5206154146820220077)
XLA Ops:
  0.6 69.6 %shard_map.94 = (bf16[256,256]{1,0:T(8,128)(2,1)}, bf16[256,2048]{1,0:T(8,128)(2,1)}, bf16[128,2048]{1,0:T(8,128)(2,1)}) custom-call(bf16[256,2048]{1,0:T(8,128)(2,1)} %text_h.1, bf16[128,2048]{1,0:T(8,128)(2,1)} %img_h.1, s32[1,256]{1,0:T(1,128)} %bitcast.4, s32[1,128]{1,0:T(1,128)} %bitcast.5, f32[1,2048]{1,0:T(1,128)} %bitcast.3, bf16[8,2048]{1,0:T(8,128)(2,1)} %w_h.1, ...), custom_call_target="tpu_custom_call" | custom-call | flops 3221225472 | bytes 6291456 | tf_op jit(solution)/shard_map/pallas_call | solution.py:513
  70.3 2.5 %shard_map.95 = (bf16[256,256]{1,0:T(8,128)(2,1)}, bf16[256,2048]{1,0:T(8,128)(2,1)}, bf16[128,2048]{1,0:T(8,128)(2,1)}) custom-call(bf16[256,256]{1,0:T(8,128)(2,1)} %get-tuple-element.6.a, bf16[256,2048]{1,0:T(8,128)(2,1)} %get-tuple-element.7.b, bf16[128,2048]{1,0:T(8,128)(2,1)} %get-tuple-element.8.c), custom_call_target="tpu_custom_call" | custom-call | tf_op jit(solution)/shard_map/pallas_call | solution.py:575

commit v6 on v5

--- a/solution.py
+++ b/solution.py
@@ -54,7 +54,7 @@
     + [(NEAR[i] + e, (e, i)) for e in STEPS for i in (1, 2)]
     + [(8, None)]
 )
-LAG1, LAG2, EXCH = 3, 6, 12
+LAG1, LAG2, EXCH = 3, 7, 12
 SLOT = {(n + 16) % 16: j for j, (n, _) in enumerate(ORDER)}
 
 

time: 72.9 us -> 72.7 us (level)
  no operation moved by 1% of the time
where the time goes in v6:
time: 72.7 us; the launch traced here: 72.6 us
  Pallas kernels  71.9 us (99%)
    pallas_call x1, Pallas kernels, per_device(): pl.pallas_call(functools.partial(kernel, nx, nz, ny), out_shape=(jax.Shap...  69.5 us
    pallas_call x1, Pallas kernels, per_device(): pl.pallas_call(flush, out_shape=tuple((jax.ShapeDtypeStruct(o.shape, o.dt...  2.45 us

profile of v6, /device:TPU:1, one launch (start us, length us, event | category | flops | bytes accessed | tf_op | source)
XLA Modules:
  0.0 72.6 jit_solution(11779525835563179945)
XLA Ops:
  0.6 69.5 %shard_map.94 = (bf16[256,256]{1,0:T(8,128)(2,1)}, bf16[256,2048]{1,0:T(8,128)(2,1)}, bf16[128,2048]{1,0:T(8,128)(2,1)}) custom-call(bf16[256,2048]{1,0:T(8,128)(2,1)} %text_h.1, bf16[128,2048]{1,0:T(8,128)(2,1)} %img_h.1, s32[1,256]{1,0:T(1,128)} %bitcast.4, s32[1,128]{1,0:T(1,128)} %bitcast.5, f32[1,2048]{1,0:T(1,128)} %bitcast.3, bf16[8,2048]{1,0:T(8,128)(2,1)} %w_h.1, ...), custom_call_target="tpu_custom_call" | custom-call | flops 3221225472 | bytes 6291456 | tf_op jit(solution)/shard_map/pallas_call | solution.py:513
  70.1 2.5 %shard_map.95 = (bf16[256,256]{1,0:T(8,128)(2,1)}, bf16[256,2048]{1,0:T(8,128)(2,1)}, bf16[128,2048]{1,0:T(8,128)(2,1)}) custom-call(bf16[256,256]{1,0:T(8,128)(2,1)} %get-tuple-element.6.a, bf16[256,2048]{1,0:T(8,128)(2,1)} %get-tuple-element.7.b, bf16[128,2048]{1,0:T(8,128)(2,1)} %get-tuple-element.8.c), custom_call_target="tpu_custom_call" | custom-call | tf_op jit(solution)/shard_map/pallas_call | solution.py:575
